TPU v7x, 32 devices: a whole 2x2x4 slice. The times are simulated.
32 devices in a mesh: patch: 16 (over z, y, x), strip: 2 (over core).
Axes of the slice: x: 2, y: 2, z: 4, core: 2. Of those that a mesh axis runs over, the one named last changes fastest.
Arguments:
- features: float32 [32768, 128], P(('patch', 'strip')), may hold values from -6 to 6
- lap_tiles: float32 [512, 6, 4096], P(('patch', 'strip')), may hold values from -0.3125 to 0.3125
- columns: int32 [512, 6], P(('patch', 'strip')), may hold values from 0 to 511, as said below
- weights: float32 [3, 64, 64], replicated, may hold values from -0.75 to 0.75
- bias_term: float32 [64], replicated, may hold values from -4 to 4
- cotangent: float32 [32768, 128], P(('patch', 'strip')), may hold values from -6 to 6
Outputs:
- output: float32 [32768, 128], P(('patch', 'strip'))
- input_grad: float32 [32768, 128], P(('patch', 'strip'))
- weight_grad: float32 [3, 64, 64], replicated
- bias_grad: float32 [64], replicated
Inputs may be any that keep to these rules, and one draw needn't show every extreme that they name: `columns`: entry 0 of a block's 6 entries is the block itself and entry 1 lies exactly 4 blocks before or after it; all entries of a block are distinct blocks within 4 of it in the cyclic order of the 512 blocks.
All inputs are finite; a program needn't handle non-finite values.
Results may differ from a plain program's by a relative error of at most 0.0001.
Values sent between devices are 32-bit elements; how exact they have to be, the bound alone decides.
A program may use at most 64 MiB of HBM per device.

v0:
```python
import math

import jax
import jax.numpy as jnp
from jax import lax
from jax.sharding import PartitionSpec as P

C = 64
BATCH = 2
PB = 64
NB = 6
HB = 4
BLK_DEV = 16


highest = lax.Precision.HIGHEST


def with_halo(cells, sides, width):
    for axis, dim in sides:
        count = lax.axis_size(axis)
        head = lax.slice_in_dim(cells, 0, width, axis=dim)
        tail = lax.slice_in_dim(cells, cells.shape[dim] - width, cells.shape[dim], axis=dim)
        cells = jnp.concatenate(
            [
                lax.ppermute(tail, axis, [(i, (i + 1) % count) for i in range(count)]),
                cells,
                lax.ppermute(head, axis, [((i + 1) % count, i) for i in range(count)]),
            ],
            axis=dim,
        )
    return cells


def passed_along(value, axis, by):
    peers = lax.axis_size(axis)
    return lax.ppermute(value, axis, [(i, (i + by) % peers) for i in range(peers)])


def lap_rows(extended, ext_first, tile_rows, column_rows, total_blocks):
    positions = jnp.mod(column_rows - ext_first, total_blocks)
    picked = extended[positions]
    tile_mats = tile_rows.reshape(tile_rows.shape[0], NB, PB, PB)
    return jnp.einsum("bjpq,bjqf->bpf", tile_mats, picked, precision=highest)


def shards(features, lap_tiles, columns, weights, bias_term, cotangent):
    row_count, feat_width = features.shape
    devices = lax.axis_size("patch") * lax.axis_size("strip")
    total_blocks = BLK_DEV * devices
    first_block = (
        lax.axis_index("patch") * lax.axis_size("strip") + lax.axis_index("strip")
    ) * BLK_DEV
    zeroth = features.reshape(BLK_DEV, PB, feat_width)

    def one_hop(field_in):
        padded = with_halo(
            field_in.reshape(row_count, feat_width), ((("patch", "strip"), 0),), HB * PB
        )
        return lap_rows(
            padded.reshape(-1, PB, feat_width), first_block - HB, lap_tiles, columns, total_blocks
        )

    first_term = one_hop(zeroth)
    second_term = 2.0 * one_hop(first_term) - zeroth
    cheb_terms = (zeroth, first_term, second_term)
    mixed_sum = bias_term
    for order_index in range(3):
        map_rows = cheb_terms[order_index].reshape(row_count, BATCH, C)
        mixed_sum = mixed_sum + jnp.einsum(
            "nbc,cd->nbd", map_rows, weights[order_index], precision=highest
        )
    output = mixed_sum.reshape(row_count, feat_width)
    grad_maps = cotangent.reshape(row_count, BATCH, C)
    back_terms = jnp.einsum("nbd,kcd->knbc", grad_maps, weights, precision=highest).reshape(
        3, BLK_DEV, PB, feat_width
    )
    tile_mats = lap_tiles.reshape(BLK_DEV, NB, PB, PB)
    positions = jnp.mod(columns - (first_block - HB), total_blocks).reshape(-1)
    slot_ids = jnp.arange(BLK_DEV + 2 * HB, dtype=jnp.int32)
    placement = (slot_ids[:, None] == positions[None, :]).astype(jnp.float32)

    def transposed(vector):
        contrib = jnp.einsum("bjpq,bpf->bjqf", tile_mats, vector, precision=highest)
        spread = jnp.dot(
            placement, contrib.reshape(BLK_DEV * NB, PB * feat_width), precision=highest
        )
        spread = spread.reshape(BLK_DEV + 2 * HB, PB, feat_width)
        low_rim = spread[:HB]
        high_rim = spread[BLK_DEV + HB :]
        from_next = passed_along(low_rim, ("patch", "strip"), -1)
        from_prev = passed_along(high_rim, ("patch", "strip"), 1)
        own_part = spread[HB : BLK_DEV + HB]
        own_part = own_part.at[:HB].add(from_prev)
        return own_part.at[BLK_DEV - HB :].add(from_next)

    inner_sum = back_terms[1] + 2.0 * transposed(back_terms[2])
    input_grad = (back_terms[0] - back_terms[2] + transposed(inner_sum)).reshape(
        row_count, feat_width
    )
    weight_local = jnp.stack(
        [
            jnp.einsum(
                "nbc,nbd->cd", term_part.reshape(row_count, BATCH, C), grad_maps, precision=highest
            )
            for term_part in cheb_terms
        ]
    )
    bias_local = jnp.sum(grad_maps, axis=(0, 1))
    weight_sum, bias_sum = lax.psum((weight_local, bias_local), ("patch", "strip"))
    grad_scale = 1.0 / math.sqrt(BATCH * PB * total_blocks)
    return (output, input_grad, weight_sum * grad_scale, bias_sum * grad_scale)


def solution(mesh):
    in_specs = (
        P(("patch", "strip"), None),
        P(("patch", "strip"), None, None),
        P(("patch", "strip"), None),
        P(),
        P(),
        P(("patch", "strip"), None),
    )
    out_specs = (P(("patch", "strip"), None), P(("patch", "strip"), None), P(), P())
    return jax.shard_map(shards, mesh=mesh, in_specs=in_specs, out_specs=out_specs, check_vma=False)
```

profile of v0, /device:TPU:0, one launch (start us, length us, event | category | flops | bytes accessed | tf_op | source)
XLA Modules:
  0.0 178.0 jit_solution(13042853195323778084)
XLA Ops:
  0.6 1.2 copy.71
  1.9 2.4 %convolution_bitcast_fusion = f32[3,1024,2,64]{1,3,2,0:T(8,128)S(1)} fusion(f32[1024,2,64,1]{0,2,1,3:T(8,128)S(1)} %bitcast.154, f32[3,64,64]{2,1,0:T(8,128)} %param.17), kind=kOutput, calls=%fused_computation.8 | convolution fusion | flops 301989888 | bytes 2146304 | tf_op jit(solution)/shard_map/nbd,kcd->knbc/dot_general | solution.py:75
  4.3 1.2 fusion.25
  5.4 1.3 squeeze.23
  6.7 3.5 %reshape.191 = f32[16,6,64,64]{3,2,0,1:T(8,128)} reshape(f32[16,6,4096]{2,0,1:T(8,128)} %param.15) | data formatting | bytes 3145728 | tf_op jit(solution)/shard_map/reshape | solution.py:43
  10.2 2.4 %copy.74 = f32[16,6,64,64]{2,3,1,0:T(8,128)S(1)} copy(f32[16,6,64,64]{3,2,0,1:T(8,128)} %reshape.191) | data formatting | bytes 3145728 | tf_op jit(solution)/shard_map/reshape | solution.py:43
  12.9 4.5 %fusion.11 = f32[16,128,384]{1,2,0:S(1)} fusion(f32[16,64,384]{1,2,0:T(8,128)S(1)} %bitcast.150, f32[16,64,128]{1,0,2:T(8,128)} %squeeze.23), kind=kOutput, calls=%fused_computation.21 | convolution fusion | flops 603979776 | bytes 5242880
  17.4 2.9 %fusion.3 = f32[24,8192]{1,0:T(8,128)S(1)} fusion(f32[12,8,64,128]{3,2,1,0:T(8,128)S(1)} %bitcast.160, s32[96]{0:T(128)S(1)} %eq.20), kind=kOutput, calls=%fused_computation.5 | convolution fusion | flops 226494720 | bytes 3932544 | tf_op jit(solution)/shard_map/dot_general | solution.py:85
  23.5 5.9 %collective-permute-start.5 = (f32[4,64,128]{1,0,2:T(4,128)}, f32[4,64,128]{1,0,2:T(4,128)}, u32[]{:S(2)}, u32[]{:S(2)}) collective-permute-start(f32[4,64,128]{1,0,2:T(4,128)} %copy.78), channel_id=1, source_target_pairs={{0,31},{1,0},{2,1},{3,2},{4,3},{5,4},{6,5},{7,6},{8,7},{9,8},{10,9... | collective-permute-start | bytes 393224 | tf_op jit(solution)/shard_map/ppermute | solution.py:37
  29.4 1.7 fusion.27
  31.1 5.3 %collective-permute-start.1 = (f32[256,128]{1,0:T(8,128)}, f32[256,128]{1,0:T(8,128)}, u32[]{:S(2)}, u32[]{:S(2)}) collective-permute-start(f32[256,128]{1,0:T(8,128)} %get-tuple-element.80), channel_id=1, source_target_pairs={{1,0},{2,1},{3,2},{4,3},{5,4},{6,5},{7,6},{8,7},{9,8},{10,9},{11,1... | collective-permute-start | bytes 393224 | tf_op jit(solution)/shard_map/ppermute | solution.py:28
  36.4 2.0 %copy.62 = f32[1024,128]{0,1:T(8,128)} copy(f32[1024,128]{1,0:T(8,128)} %param.14) | data formatting | bytes 1048576 | tf_op args[0]
  38.5 2.4 %convolution_bitcast_fusion.4 = f32[1,64,64]{2,1,0:T(8,128)} fusion(f32[1024,2,64]{0,2,1:T(8,128)} %bitcast.166, f32[1024,2,64]{0,2,1:T(8,128)} %bitcast.155), kind=kOutput, calls=%fused_computation.18 | convolution fusion | flops 100663296 | bytes 1064960 | tf_op jit(solution)/shard_map/nbc,nbd->cd/dot_general | solution.py:103
  40.9 2.5 %convolution_add_fusion.2 = f32[1024,2,64]{0,2,1:T(8,128)} fusion(f32[1024,2,64]{0,2,1:T(8,128)} %bitcast.167, f32[64]{0:T(128)S(1)} %copy-done.11, f32[3,64,64]{2,1,0:T(8,128)} %param.17), kind=kOutput, calls=%fused_computation.12 | convolution fusion | flops 100794368 | bytes 1081600 | tf_op jit(solution)/shard_map/nbc,cd->nbd/dot_general | solution.py:70
  43.3 2.0 %slice_bitcast_fusion.1 = f32[2,8,64,128]{3,1,2,0:T(8,128)} fusion(f32[24,8192]{1,0:T(8,128)} %copy-done.6), kind=kLoop, calls=%fused_computation.28 | loop fusion | bytes 1048576
  45.5 2.0 %copy.96 = f32[2,8,64,128]{3,2,1,0:T(8,128)} copy(f32[2,8,64,128]{3,1,2,0:T(8,128)} %slice_bitcast_fusion.1) | data formatting | bytes 1048576
  47.4 2.4 %copy.77 = f32[16,64,128]{1,0,2:T(8,128)} copy(f32[16,64,128]{2,1,0:T(8,128)} %bitcast.169) | data formatting | bytes 1048576 | tf_op jit(solution)/shard_map/slice | solution.py:93
  49.8 2.3 %squeeze.24 = f32[16,64,128]{1,0,2:T(8,128)} reshape(f32[1,1024,2,64]{1,3,2,0:T(8,128)} %get-tuple-element.69) | data formatting | bytes 1048576 | tf_op jit(solution)/shard_map/squeeze | solution.py:97
  52.1 2.3 %squeeze.22 = f32[16,64,128]{1,0,2:T(8,128)} reshape(f32[1,1024,2,64]{1,3,2,0:T(8,128)} %get-tuple-element.68) | data formatting | bytes 1048576 | tf_op jit(solution)/shard_map/squeeze | solution.py:98
  54.6 1.2 reduce_sum.10
  55.9 1.8 add_dynamic-update-slice_fusion.1
  57.7 1.9 %fusion.14 = f32[16,64,128]{1,0,2:T(8,128)} fusion(f32[16,64,128]{1,0,2:T(8,128)} %add_dynamic-update-slice_fusion.1, f32[4,64,128]{1,0,2:T(4,128)} %collective-permute-done.5), kind=kLoop, calls=%fused_computation.32 | loop fusion | flops 32768 | bytes 786432 | tf_op jit(solution)/shard_map/scatter-add | solution.py:95
  59.6 1.7 multiply_add_fusion
  61.3 3.3 %fusion.9 = f32[16,128,384]{1,2,0:S(1)} fusion(f32[16,64,384]{1,2,0:T(8,128)S(1)} %bitcast.151, f32[16,64,128]{1,0,2:T(8,128)S(1)} %multiply_add_fusion), kind=kOutput, calls=%fused_computation.19 | convolution fusion | flops 603979776 | bytes 5242880
  64.6 2.9 %fusion = f32[24,8192]{1,0:T(8,128)S(1)} fusion(f32[12,8,64,128]{3,2,1,0:T(8,128)S(1)} %bitcast.159, s32[96]{0:T(128)S(1)} %eq.20), kind=kOutput, calls=%fused_computation.2 | convolution fusion | flops 226494720 | bytes 3932544 | tf_op jit(solution)/shard_map/dot_general | solution.py:85
  69.1 1.9 %pad_maximum_fusion = f32[1536,128]{1,0:T(8,128)} fusion(f32[256,128]{1,0:T(8,128)} %collective-permute-done.1, f32[1024,128]{1,0:T(8,128)S(1)} %copy-done.3, f32[256,128]{1,0:T(8,128)} %collective-permute-done), kind=kLoop, calls=%fused_computation.25 | loop fusion | flops 393216 | bytes 1572864 | tf_op jit(solution)/shard_map/concatenate | solution.py:24
  71.1 3.5 %gather_fusion = f32[96,64,128]{2,1,0:T(8,128)} fusion(f32[24,64,128]{2,1,0:T(8,128)} %bitcast.153, s32[1024]{0:T(1024)S(1)} %pad_clamp_fusion), kind=kCustom, calls=%fused_computation | custom fusion | bytes 6291840 | tf_op jit(solution)/shard_map/gather | solution.py:42
  74.6 7.4 %fusion.28 = f32[16,128,64,1]{1,2,3,0:T(8,128)S(1)} fusion(f32[16,6,64,128]{3,2,1,0:T(8,128)} %bitcast.161, f32[16,6,64,64]{2,3,1,0:T(8,128)S(1)} %copy.74), kind=kOutput, calls=%fused_computation.69 | convolution fusion | flops 603979776 | bytes 5242880 | tf_op jit(solution)/shard_map/bjpq,bjqf->bpf/dot_general | solution.py:44
  83.5 2.6 %reshape.238 = f32[1024,2,64]{2,1,0:T(2,128)} reshape(f32[16,64,128]{2,1,0:T(8,128)} %bitcast.164) | data formatting | bytes 1048576 | tf_op jit(solution)/shard_map/reshape | solution.py:69
  87.2 1.9 %copy.101 = f32[2,8,64,128]{3,2,1,0:T(8,128)} copy(f32[2,8,64,128]{3,1,2,0:T(8,128)} %slice_bitcast_fusion) | data formatting | bytes 1048576
  89.2 2.4 %copy.83 = f32[16,64,128]{1,0,2:T(8,128)} copy(f32[16,64,128]{2,1,0:T(8,128)} %bitcast.170) | data formatting | bytes 1048576 | tf_op jit(solution)/shard_map/slice | solution.py:93
  91.6 0.9 copy.123
  93.4 5.3 %collective-permute-start.7 = (f32[4,64,128]{1,0,2:T(4,128)}, f32[4,64,128]{1,0,2:T(4,128)}, u32[]{:S(2)}, u32[]{:S(2)}) collective-permute-start(f32[4,64,128]{1,0,2:T(4,128)} %copy.84), channel_id=1, source_target_pairs={{0,31},{1,0},{2,1},{3,2},{4,3},{5,4},{6,5},{7,6},{8,7},{9,8},{10,9... | collective-permute-start | bytes 393224 | tf_op jit(solution)/shard_map/ppermute | solution.py:37
  98.7 5.3 %collective-permute-start.3 = (f32[256,128]{1,0:T(8,128)}, f32[256,128]{1,0:T(8,128)}, u32[]{:S(2)}, u32[]{:S(2)}) collective-permute-start(f32[256,128]{1,0:T(8,128)} %bitcast.178), channel_id=1, source_target_pairs={{1,0},{2,1},{3,2},{4,3},{5,4},{6,5},{7,6},{8,7},{9,8},{10,9},{11,1... | collective-permute-start | bytes 393224 | tf_op jit(solution)/shard_map/ppermute | solution.py:28
  104.0 2.1 %copy.90 = f32[1024,2,64]{0,2,1:T(8,128)} copy(f32[1024,2,64]{2,1,0:T(2,128)} %reshape.238) | data formatting | bytes 1048576 | tf_op jit(solution)/shard_map/reshape | solution.py:69
  106.2 2.8 %convolution_add_fusion.1 = f32[1024,2,64]{0,2,1:T(8,128)} fusion(f32[1024,2,64]{0,2,1:T(8,128)} %convolution_add_fusion.2, f32[1024,2,64]{0,2,1:T(8,128)} %copy.90, f32[3,64,64]{2,1,0:T(8,128)} %param.17), kind=kOutput, calls=%fused_computation.11 | convolution fusion | flops 100794368 | bytes 1605632 | tf_op jit(solution)/shard_map/nbc,cd->nbd/dot_general | solution.py:70
  109.0 2.4 %convolution_bitcast_fusion.3 = f32[1,64,64]{2,1,0:T(8,128)} fusion(f32[1024,2,64]{0,2,1:T(8,128)} %copy.90, f32[1024,2,64]{0,2,1:T(8,128)} %bitcast.156), kind=kOutput, calls=%fused_computation.17 | convolution fusion | flops 100663296 | bytes 1064960 | tf_op jit(solution)/shard_map/nbc,nbd->cd/dot_general | solution.py:103
  111.3 1.8 add_dynamic-update-slice_fusion
  113.1 1.9 %fusion.13 = f32[16,64,128]{1,0,2:T(8,128)} fusion(f32[16,64,128]{1,0,2:T(8,128)} %add_dynamic-update-slice_fusion, f32[4,64,128]{1,0,2:T(4,128)} %collective-permute-done.7), kind=kLoop, calls=%fused_computation.30 | loop fusion | flops 32768 | bytes 786432 | tf_op jit(solution)/shard_map/scatter-add | solution.py:95
  115.1 2.4 %subtract_add_fusion = f32[16,64,128]{1,0,2:T(8,128)} fusion(f32[16,64,128]{1,0,2:T(8,128)} %fusion.13, f32[16,64,128]{1,0,2:T(8,128)S(1)} %copy-done.5, f32[16,64,128]{1,0,2:T(8,128)S(1)} %copy-done.2), kind=kLoop, calls=%fused_computation.24 | loop fusion | flops 262144 | bytes 2097152 | tf_op jit(solution)/shard_map/add | solution.py:98
  117.5 2.4 %copy.85 = f32[16,64,128]{2,1,0:T(8,128)} copy(f32[16,64,128]{1,0,2:T(8,128)} %subtract_add_fusion) | data formatting | bytes 1048576 | tf_op jit(solution)/shard_map/add | solution.py:98
  119.9 2.1 %pad_maximum_fusion.1 = f32[1536,128]{1,0:T(8,128)} fusion(f32[256,128]{1,0:T(8,128)} %collective-permute-done.3, f32[1024,128]{1,0:T(8,128)} %bitcast.165, f32[256,128]{1,0:T(8,128)S(1)} %collective-permute-done.2), kind=kLoop, calls=%fused_computation.26 | loop fusion | flops 393216 | bytes 1572864 | tf_op jit(solution)/shard_map/concatenate | solution.py:24
  121.9 3.5 %gather_fusion.1 = f32[96,64,128]{2,1,0:T(8,128)} fusion(f32[24,64,128]{2,1,0:T(8,128)} %bitcast.152, s32[1024]{0:T(1024)S(1)} %pad_clamp_fusion), kind=kCustom, calls=%fused_computation.1 | custom fusion | bytes 6291840 | tf_op jit(solution)/shard_map/gather | solution.py:42
  125.5 8.1 %fusion.8 = f32[16,64,128]{2,1,0:T(8,128)} fusion(f32[16,64,128]{2,1,0:T(8,128)} %bitcast.162, f32[16,6,64,128]{3,2,1,0:T(8,128)} %bitcast.158, f32[16,6,64,64]{2,3,1,0:T(8,128)S(1)} %copy.74), kind=kOutput, calls=%fused_computation.15 | convolution fusion | flops 604241920 | bytes 5767168 | tf_op jit(solution)/shard_map/bjpq,bjqf->bpf/dot_general | solution.py:44
  133.5 1.7 reshape.239
  136.4 38.0 %all-reduce = (f32[3,64,64]{2,1,0:T(8,128)S(1)}, f32[64]{0:T(128)S(1)}) all-reduce(f32[3,64,64]{2,1,0:T(8,128)S(1)} %pad_maximum_fusion.2, f32[64]{0:T(128)S(1)} %reduce_sum.18), channel_id=1, replica_groups=mesh['patch'=16,'strip'=2] {'patch','strip'}, use_global_device_ids=true, to_apply=%region_0.1 | all-reduce | flops 12352 | bytes 98816 | tf_op jit(solution)/shard_map/psum | solution.py:110
  175.6 1.4 convolution_add_fusion
  177.0 1.0 copy.86
  (64 shorter events, 11.0 us)
Async XLA Ops:
  1.9 4.8 %copy-start = (f32[1024,128]{0,1:T(8,128)}, f32[1024,128]{0,1:T(8,128)S(1)}, u32[]{:S(2)}) copy-start(f32[1024,128]{0,1:T(8,128)S(1)} %copy.71) | copy-start | bytes 1572868
  10.2 2.4 %copy-start.10 = (s32[16,6]{0,1:T(8,128)S(1)}, s32[16,6]{0,1:T(8,128)}, u32[]{:S(2)}) copy-start(s32[16,6]{0,1:T(8,128)} %param.16) | copy-start | bytes 1156
  20.3 0.9 copy-start.6
  21.2 19.6 %copy-start.11 = (f32[64]{0:T(128)S(1)}, f32[64]{0:T(128)}, u32[]{:S(2)}) copy-start(f32[64]{0:T(128)} %param.18) | copy-start | bytes 772
  22.2 33.8 %collective-permute-start.4 = (f32[4,64,128]{1,0,2:T(4,128)}, f32[4,64,128]{1,0,2:T(4,128)}, u32[]{:S(2)}, u32[]{:S(2)}) collective-permute-start(f32[4,64,128]{1,0,2:T(4,128)} %copy.75), channel_id=1, source_target_pairs={{0,1},{1,2},{2,3},{3,4},{4,5},{5,6},{6,7},{7,8},{8,9},{9,10},{10,1... | collective-permute-start | bytes 393224 | tf_op jit(solution)/shard_map/ppermute | solution.py:37
  23.5 34.2 %collective-permute-start.5 = (f32[4,64,128]{1,0,2:T(4,128)}, f32[4,64,128]{1,0,2:T(4,128)}, u32[]{:S(2)}, u32[]{:S(2)}) collective-permute-start(f32[4,64,128]{1,0,2:T(4,128)} %copy.78), channel_id=1, source_target_pairs={{0,31},{1,0},{2,1},{3,2},{4,3},{5,4},{6,5},{7,6},{8,7},{9,8},{10,9... | collective-permute-start | bytes 393224 | tf_op jit(solution)/shard_map/ppermute | solution.py:37
  31.1 38.0 %collective-permute-start = (f32[256,128]{1,0:T(8,128)}, f32[256,128]{1,0:T(8,128)}, u32[]{:S(2)}, u32[]{:S(2)}) collective-permute-start(f32[256,128]{1,0:T(8,128)} %get-tuple-element.79), channel_id=1, source_target_pairs={{0,1},{1,2},{2,3},{3,4},{4,5},{5,6},{6,7},{7,8},{8,9},{9,10},{10,1... | collective-permute-start | bytes 393224 | tf_op jit(solution)/shard_map/ppermute | solution.py:26
  31.1 38.0 %collective-permute-start.1 = (f32[256,128]{1,0:T(8,128)}, f32[256,128]{1,0:T(8,128)}, u32[]{:S(2)}, u32[]{:S(2)}) collective-permute-start(f32[256,128]{1,0:T(8,128)} %get-tuple-element.80), channel_id=1, source_target_pairs={{1,0},{2,1},{3,2},{4,3},{5,4},{6,5},{7,6},{8,7},{9,8},{10,9},{11,1... | collective-permute-start | bytes 393224 | tf_op jit(solution)/shard_map/ppermute | solution.py:28
  64.6 4.5 %copy-start.3 = (f32[1024,128]{1,0:T(8,128)S(1)}, f32[1024,128]{1,0:T(8,128)}, u32[]{:S(2)}) copy-start(f32[1024,128]{1,0:T(8,128)} %param.14) | copy-start | bytes 1572868
  82.0 0.8 copy-start.4
  87.0 24.3 %collective-permute-start.6 = (f32[4,64,128]{1,0,2:T(4,128)}, f32[4,64,128]{1,0,2:T(4,128)}, u32[]{:S(2)}, u32[]{:S(2)}) collective-permute-start(f32[4,64,128]{1,0,2:T(4,128)} %copy.81), channel_id=1, source_target_pairs={{0,1},{1,2},{2,3},{3,4},{4,5},{5,6},{6,7},{7,8},{8,9},{9,10},{10,1... | collective-permute-start | bytes 393224 | tf_op jit(solution)/shard_map/ppermute | solution.py:37
  93.4 19.7 %collective-permute-start.7 = (f32[4,64,128]{1,0,2:T(4,128)}, f32[4,64,128]{1,0,2:T(4,128)}, u32[]{:S(2)}, u32[]{:S(2)}) collective-permute-start(f32[4,64,128]{1,0,2:T(4,128)} %copy.84), channel_id=1, source_target_pairs={{0,31},{1,0},{2,1},{3,2},{4,3},{5,4},{6,5},{7,6},{8,7},{9,8},{10,9... | collective-permute-start | bytes 393224 | tf_op jit(solution)/shard_map/ppermute | solution.py:37
  98.7 21.2 %collective-permute-start.2 = (f32[256,128]{1,0:T(8,128)}, f32[256,128]{1,0:T(8,128)S(1)}, u32[]{:S(2)}, u32[]{:S(2)}) collective-permute-start(f32[256,128]{1,0:T(8,128)} %bitcast.179), channel_id=1, source_target_pairs={{0,1},{1,2},{2,3},{3,4},{4,5},{5,6},{6,7},{7,8},{8,9},{9,10},{10,1... | collective-permute-start | bytes 393224 | tf_op jit(solution)/shard_map/ppermute | solution.py:26
  98.7 21.2 %collective-permute-start.3 = (f32[256,128]{1,0:T(8,128)}, f32[256,128]{1,0:T(8,128)}, u32[]{:S(2)}, u32[]{:S(2)}) collective-permute-start(f32[256,128]{1,0:T(8,128)} %bitcast.178), channel_id=1, source_target_pairs={{1,0},{2,1},{3,2},{4,3},{5,4},{6,5},{7,6},{8,7},{9,8},{10,9},{11,1... | collective-permute-start | bytes 393224 | tf_op jit(solution)/shard_map/ppermute | solution.py:28
  106.2 8.9 %copy-start.2 = (f32[16,64,128]{1,0,2:T(8,128)S(1)}, f32[16,64,128]{1,0,2:T(8,128)}, u32[]{:S(2)}) copy-start(f32[16,64,128]{1,0,2:T(8,128)} %squeeze.23) | copy-start | bytes 1572868
  106.2 8.9 %copy-start.5 = (f32[16,64,128]{1,0,2:T(8,128)S(1)}, f32[16,64,128]{1,0,2:T(8,128)}, u32[]{:S(2)}) copy-start(f32[16,64,128]{1,0,2:T(8,128)} %squeeze.22) | copy-start | bytes 1572868
  133.5 2.3 %copy-start.1 = (f32[1024,128]{0,1:T(8,128)S(1)}, f32[1024,128]{0,1:T(8,128)}, u32[]{:S(2)}) copy-start(f32[1024,128]{0,1:T(8,128)} %copy-done) | copy-start | bytes 1572868
  133.5 2.8 %copy-start.8 = (f32[1,64,64]{2,1,0:T(8,128)S(1)}, f32[1,64,64]{2,1,0:T(8,128)}, u32[]{:S(2)}) copy-start(f32[1,64,64]{2,1,0:T(8,128)} %convolution_bitcast_fusion.4) | copy-start | bytes 49156
  133.5 2.8 %copy-start.9 = (f32[1,64,64]{2,1,0:T(8,128)S(1)}, f32[1,64,64]{2,1,0:T(8,128)}, u32[]{:S(2)}) copy-start(f32[1,64,64]{2,1,0:T(8,128)} %convolution_bitcast_fusion.3) | copy-start | bytes 49156
  133.5 42.0 %copy-start.7 = (f32[1024,2,64]{0,2,1:T(8,128)S(1)}, f32[1024,2,64]{0,2,1:T(8,128)}, u32[]{:S(2)}) copy-start(f32[1024,2,64]{0,2,1:T(8,128)} %convolution_add_fusion.1) | copy-start | bytes 1572868
where the time goes:
time: 180 us; the launch traced here: 178 us
  local copies, waits for them, and re-layouts  55.3 us (31%)
  matrix products  43.4 us (24%)
  blocking collectives  38 us (21%)
  starting transfers between devices  22.4 us (12%)
  other arithmetic  17.9 us (10%)
    psum x1, blocking collectives, shards(): lax.psum((weight_local, bias_local), ('patch', 'strip'))  38 us
    dot_general x2, matrix products, lap_rows(): return jnp.einsum('bjpq,bjqf->bpf', tile_mats, picked, precision=highest)  15.4 us
    unnamed x39, local copies, waits for them, and re-layouts  14.5 us
    ppermute x4, starting transfers between devices, passed_along(): lax.ppermute(value, axis, [(i, (i + by) % peers) for i in range(peers)])  11.7 us
    ppermute x2, starting transfers between devices, with_halo(): lax.ppermute(head, axis, [((i + 1) % count, i) for i in range(count)])  10.7 us
    unnamed x2, matrix products  7.83 us
    gather x2, local copies, waits for them, and re-layouts, lap_rows(): picked = extended[positions]  7.05 us
    reshape x4, local copies, waits for them, and re-layouts, shards(): map_rows = cheb_terms[order_index].reshape(row_count, BATCH, C)  6.98 us
  transfers between devices with their start and end apart: 8, of which 0 were waited for; matrix products, arithmetic and copies ran while one was open for 32% of the time, Pallas kernels for 0%

commit v1 on v0

v1 whole, which is shorter than its diff:
```python
import functools
import math

import jax
import jax.numpy as jnp
from jax import lax
from jax.experimental import pallas as pl
from jax.experimental.pallas import tpu as pltpu
from jax.sharding import PartitionSpec as P

MESH = pl.DeviceIdType.MESH
PEERS = 8
f32, bf16 = jnp.float32, jnp.bfloat16


def halves(x):
    hi = x.astype(bf16)
    return hi, (x - hi.astype(f32)).astype(bf16)


def dot(a, b):
    return jnp.dot(a, b, preferred_element_type=f32)


def side_by_side(x):
    return jnp.concatenate(halves(x), axis=1)


def stacked(x):
    return jnp.concatenate(halves(x), axis=0)


def both_maps(w):
    zero = jnp.zeros_like(w)
    return jnp.concatenate(
        [jnp.concatenate([w, zero], axis=1), jnp.concatenate([zero, w], axis=1)], axis=0
    )


def body(
    dims,
    f_hbm, lap_hbm, col, w_ref, b_ref, cot_hbm,
    out_hbm, ig_hbm, wg_ref, bg_ref,
    f_v, cot_v, lap_v, y, dhi, dlo, fc, tc, cc, uc, wf, wb, out_v, ig_v,
    f_in, t_in, u_in, v_in, t_out, u_out, v_out,
    grads, part_in, seg, cross, final,
    send, recv, a_send, a_recv, b_send, b_recv, c_send, c_recv, local, put,
):
    nb, pb, blocks, hb, total, scale = dims
    half, width = hb * pb, f_v.shape[1]
    rows = blocks * pb
    groups = blocks // hb
    chan = width // 2
    strips = lax.axis_size("strip")
    n = lax.axis_size("patch") * strips
    me = lax.axis_index("patch") * strips + lax.axis_index("strip")
    first = me * blocks
    teams = n // PEERS
    team, rank = me // PEERS, me % PEERS

    def at(index):
        return (index // strips, index % strips)

    prev, nxt = at((me + n - 1) % n), at((me + 1) % n)
    mates = [(rank + o) % PEERS for o in range(1, PEERS)]
    others = [(team + o) % teams for o in range(1, teams)]

    barrier = pltpu.get_barrier_semaphore()
    greeted = [prev, nxt]
    greeted += [at(team * PEERS + m) for m in mates]
    greeted += [at(t * PEERS + rank) for t in others]
    for device in greeted:
        pl.semaphore_signal(barrier, inc=1, device_id=device, device_id_type=MESH)
    load_lap = pltpu.make_async_copy(lap_hbm, lap_v, local.at[0])
    load_cot = pltpu.make_async_copy(cot_hbm, cot_v, local.at[1])
    load_f = pltpu.make_async_copy(f_hbm, f_v, local.at[2])
    load_lap.start()
    load_cot.start()
    load_f.start()
    pl.semaphore_wait(barrier, len(greeted))

    def swap(slot, to_next, to_prev, landing):
        pair = []
        for i, (src, device) in enumerate(((to_next, nxt), (to_prev, prev))):
            copy = pltpu.make_async_remote_copy(
                src_ref=src,
                dst_ref=landing.at[i],
                send_sem=send.at[2 * slot + i],
                recv_sem=recv.at[2 * slot + i],
                device_id=device,
                device_id_type=MESH,
            )
            copy.start()
            pair.append(copy)
        return pair

    f_swap = swap(0, f_hbm.at[pl.ds(rows - half, half)], f_hbm.at[pl.ds(0, half)], f_in)

    load_lap.wait()
    low = lax.broadcasted_iota(jnp.int32, (8, 128), 1) < pb

    def spread(j, carry):
        for eight in range(blocks // 8):
            for r in range(pb // 2):
                x = lap_v[j, pl.ds(8 * eight, 8), pl.ds(128 * r, 128)]
                turned = pltpu.roll(x, 64, 1)
                start = 8 * eight * nb * pb + j * pb + 2 * r
                y[pl.ds(start, 8, stride=nb * pb), :] = jnp.where(low, x, turned)
                y[pl.ds(start + 1, 8, stride=nb * pb), :] = jnp.where(low, turned, x)
        return carry

    lax.fori_loop(0, nb, spread, 0)

    side = lax.broadcasted_iota(jnp.int32, (pb, 128), 1) // pb

    def band(g, carry):
        for i in range(hb):
            b = g * hb + i
            spots = []
            for j in range(nb):
                d = col[j, b] - (first + b - hb)
                d = jnp.where(d < 0, d + total, d)
                d = jnp.where(d >= total, d - total, d)
                spots.append(d + i)
            own = pl.ds(pl.multiple_of(b * pb, pb), pb)
            for m in range(3 * hb // 2):
                columns = pl.ds(128 * m, 128)
                if 2 * m + 1 < i or 2 * m > i + 2 * hb:
                    dhi[own, columns] = jnp.zeros((pb, 128), bf16)
                    dlo[own, columns] = jnp.zeros((pb, 128), bf16)
                    continue
                picked = jnp.zeros((pb, 128), f32)
                for j in range(nb):
                    tile = y[pl.ds(pl.multiple_of((b * nb + j) * pb, pb), pb), :]
                    picked = jnp.where(side + 2 * m == spots[j], tile, picked)
                hi, lo = halves(picked)
                dhi[own, columns] = hi
                dlo[own, columns] = lo
        return carry

    lax.fori_loop(0, 2, lambda t, carry: band(t * (groups - 1), carry), 0)

    load_cot.wait()
    for g in range(groups):
        cc[:, pl.ds(g * half, half)] = stacked(cot_v[pl.ds(g * half, half), :].T)

    def hop(g, field):
        own = pl.ds(g * half, half)
        near = field[pl.ds(g * half, 3 * half), :]
        both = dot(dhi[own, :], near)
        return both[:, :width] + both[:, width:] + dot(dlo[own, :], near[:, :width])

    def back_hop(k, field):
        total_here = None
        for g in range(max(0, k - 2), min(groups - 1, k) + 1):
            value = field[:, pl.ds(g * half, half)]
            block = (pl.ds(g * half, half), pl.ds((k - g) * half, half))
            both = dot(value, dhi[block])
            term = both[:width] + both[width:] + dot(value[:width], dlo[block])
            total_here = term if total_here is None else total_here + term
        return total_here

    u_out[0] = back_hop(groups + 1, cc)
    u_out[1] = back_hop(0, cc)
    u_swap = swap(1, u_out.at[0], u_out.at[1], u_in)

    lax.fori_loop(1, groups - 1, band, 0)
    load_f.wait()
    fc[pl.ds(half, rows), :] = side_by_side(f_v[...])

    for copy in f_swap:
        copy.wait_recv()
    fc[pl.ds(0, half), :] = side_by_side(f_in[0])
    fc[pl.ds(half + rows, half), :] = side_by_side(f_in[1])
    for slot, g in ((0, groups - 1), (1, 0)):
        first_term = hop(g, fc)
        t_out[slot] = first_term
        tc[pl.ds((g + 1) * half, half), :] = side_by_side(first_term)
    t_swap = swap(2, t_out.at[0], t_out.at[1], t_in)

    for copy in u_swap:
        copy.wait_recv()
    for slot, k in ((0, 1), (1, groups)):
        uc[:, pl.ds((k - 1) * half, half)] = stacked(back_hop(k, cc) + u_in[slot])
    v_out[0] = back_hop(groups + 1, uc)
    v_out[1] = back_hop(0, uc)
    v_swap = swap(3, v_out.at[0], v_out.at[1], v_in)

    for g in range(1, groups - 1):
        tc[pl.ds((g + 1) * half, half), :] = side_by_side(hop(g, fc))
        uc[:, pl.ds(g * half, half)] = stacked(back_hop(g + 1, cc))

    def share(left, right):
        whole = dot(left[...], right[pl.ds(half, rows), :])
        whole = (whole[:width, :width] + whole[width:, width:]) + (
            whole[:width, width:] + whole[width:, :width]
        )
        whole = whole.T
        return whole[:chan] + pltpu.roll(whole[chan:], chan, 1)

    zeroth, one, two = share(cc, fc), share(cc, tc), share(uc, tc)
    left_lanes = lax.broadcasted_iota(jnp.int32, (chan, width), 1) < chan
    top_row = lax.broadcasted_iota(jnp.int32, (chan, width), 0) == 0
    bias_row = jnp.sum(cot_v[...], axis=0, keepdims=True)
    bias_row = bias_row + pltpu.roll(jnp.broadcast_to(bias_row, (8, width)), chan, 1)[:1]
    first_pair = jnp.where(left_lanes, zeroth, pltpu.roll(one, chan, 1))
    second_pair = jnp.where(
        left_lanes, 2.0 * two - zeroth, jnp.where(top_row, bias_row, 0.0)
    )
    rim = 2 * chan // PEERS
    for s in range(PEERS):
        source = first_pair if s < PEERS // 2 else second_pair
        start = (s % (PEERS // 2)) * rim
        grads[s] = source[start : start + rim]
    a_copies = []
    for o, m in enumerate(mates):
        copy = pltpu.make_async_remote_copy(
            src_ref=grads.at[m],
            dst_ref=part_in.at[o],
            send_sem=a_send.at[o],
            recv_sem=a_recv.at[o],
            device_id=at(team * PEERS + m),
            device_id_type=MESH,
        )
        copy.start()
        a_copies.append(copy)

    w0, w1, w2 = w_ref[0], w_ref[1], w_ref[2]
    for k, mixing in enumerate((w0 - w2, w1, 2.0 * w2)):
        hi, lo = halves(both_maps(mixing))
        zero = jnp.zeros_like(lo)
        wf[k] = jnp.concatenate(
            [jnp.concatenate([hi, lo], axis=1), jnp.concatenate([hi, zero], axis=1)], axis=0
        )
        wb[k] = jnp.concatenate(
            [jnp.concatenate([hi, hi], axis=1), jnp.concatenate([lo, zero], axis=1)], axis=0
        )
    bias = jnp.concatenate([b_ref[...], b_ref[...]], axis=1)
    puts = []

    def finish_out(g):
        own = pl.ds((g + 1) * half, half)
        both = dot(fc[own, :], wf[0]) + dot(tc[own, :], wf[1])
        both = both + dot(side_by_side(hop(g, tc)), wf[2])
        here = pl.ds(g * half, half)
        out_v[here, :] = both[:, :width] + both[:, width:] + bias
        copy = pltpu.make_async_copy(out_v.at[here], out_hbm.at[here], put.at[g])
        copy.start()
        puts.append(copy)

    def finish_grad(g, arrived):
        here = pl.ds(g * half, half)
        second = back_hop(g + 1, uc)
        if arrived is not None:
            second = second + arrived
        both = dot(wb[0], cc[:, here]) + dot(wb[1], uc[:, here]) + dot(wb[2], stacked(second))
        ig_v[here, :] = (both[:width] + both[width:]).T
        copy = pltpu.make_async_copy(ig_v.at[here], ig_hbm.at[here], put.at[groups + g])
        copy.start()
        puts.append(copy)

    for g in range(1, groups - 1):
        finish_out(g)
        finish_grad(g, None)

    for copy in a_copies:
        copy.wait_recv()
    summed = grads[rank]
    for o in range(PEERS - 1):
        summed = summed + part_in[o]
    seg[...] = summed
    cross[team] = summed
    b_copies = []
    for o, t in enumerate(others):
        copy = pltpu.make_async_remote_copy(
            src_ref=seg,
            dst_ref=cross.at[team],
            send_sem=b_send.at[o],
            recv_sem=b_recv.at[o],
            device_id=at(t * PEERS + rank),
            device_id_type=MESH,
        )
        copy.start()
        b_copies.append(copy)

    for copy in t_swap:
        copy.wait_recv()
    tc[pl.ds(0, half), :] = side_by_side(t_in[0])
    tc[pl.ds(half + rows, half), :] = side_by_side(t_in[1])
    finish_out(0)
    finish_out(groups - 1)

    for copy in b_copies:
        copy.wait_recv()
    summed = cross[0]
    for t in range(1, teams):
        summed = summed + cross[t]
    summed = summed * scale
    final[rank] = summed
    for copy in b_copies:
        copy.wait_send()
    seg[...] = summed
    c_copies = []
    for o, m in enumerate(mates):
        copy = pltpu.make_async_remote_copy(
            src_ref=seg,
            dst_ref=final.at[rank],
            send_sem=c_send.at[o],
            recv_sem=c_recv.at[o],
            device_id=at(team * PEERS + m),
            device_id_type=MESH,
        )
        copy.start()
        c_copies.append(copy)

    for copy in v_swap:
        copy.wait_recv()
    finish_grad(0, v_in[0])
    finish_grad(groups - 1, v_in[1])

    for copy in c_copies:
        copy.wait_recv()
    for s in range(PEERS):
        piece = final[s]
        start = (s % (PEERS // 2)) * rim
        if s < PEERS // 2:
            wg_ref[0, pl.ds(start, rim), :] = piece[:, :chan]
            wg_ref[1, pl.ds(start, rim), :] = piece[:, chan:]
        else:
            wg_ref[2, pl.ds(start, rim), :] = piece[:, :chan]
    bg_ref[...] = final[PEERS // 2][:1, chan:]

    for copy in f_swap + u_swap + t_swap + v_swap + a_copies + c_copies:
        copy.wait_send()
    for copy in puts:
        copy.wait()


def shards(features, lap_tiles, columns, weights, bias_term, cotangent):
    rows, width = features.shape
    blocks, nb, tile = lap_tiles.shape
    pb = math.isqrt(tile)
    hb = 4
    half = hb * pb
    chan = width // 2
    devices = lax.axis_size("patch") * lax.axis_size("strip")
    teams = devices // PEERS
    rim = 2 * chan // PEERS
    groups = blocks // hb
    scale = 1.0 / math.sqrt(2 * rows * devices)
    vmem = pl.BlockSpec(memory_space=pltpu.VMEM)
    any_space = pl.BlockSpec(memory_space=pl.ANY)
    dma = pltpu.SemaphoreType.DMA
    output, input_grad, weight_grad, bias_grad = pl.pallas_call(
        functools.partial(body, (nb, pb, blocks, hb, blocks * devices, scale)),
        out_shape=(
            jax.ShapeDtypeStruct((rows, width), f32),
            jax.ShapeDtypeStruct((rows, width), f32),
            jax.ShapeDtypeStruct((3, chan, chan), f32),
            jax.ShapeDtypeStruct((1, chan), f32),
        ),
        in_specs=[
            any_space,
            any_space,
            pl.BlockSpec(memory_space=pltpu.SMEM),
            vmem,
            vmem,
            any_space,
        ],
        out_specs=(any_space, any_space, vmem, vmem),
        scratch_shapes=[
            pltpu.VMEM((rows, width), f32),
            pltpu.VMEM((rows, width), f32),
            pltpu.VMEM((nb, blocks, tile), f32),
            pltpu.VMEM((blocks * nb * pb, 128), f32),
            pltpu.VMEM((rows, 3 * half), bf16),
            pltpu.VMEM((rows, 3 * half), bf16),
            pltpu.VMEM((rows + 2 * half, 2 * width), bf16),
            pltpu.VMEM((rows + 2 * half, 2 * width), bf16),
            pltpu.VMEM((2 * width, rows), bf16),
            pltpu.VMEM((2 * width, rows), bf16),
            pltpu.VMEM((3, 2 * width, 2 * width), bf16),
            pltpu.VMEM((3, 2 * width, 2 * width), bf16),
            pltpu.VMEM((rows, width), f32),
            pltpu.VMEM((rows, width), f32),
            pltpu.VMEM((2, half, width), f32),
            pltpu.VMEM((2, half, width), f32),
            pltpu.VMEM((2, width, half), f32),
            pltpu.VMEM((2, width, half), f32),
            pltpu.VMEM((2, half, width), f32),
            pltpu.VMEM((2, width, half), f32),
            pltpu.VMEM((2, width, half), f32),
            pltpu.VMEM((PEERS, rim, width), f32),
            pltpu.VMEM((PEERS - 1, rim, width), f32),
            pltpu.VMEM((rim, width), f32),
            pltpu.VMEM((teams, rim, width), f32),
            pltpu.VMEM((PEERS, rim, width), f32),
            dma((8,)),
            dma((8,)),
            dma((PEERS - 1,)),
            dma((PEERS - 1,)),
            dma((teams - 1,)),
            dma((teams - 1,)),
            dma((PEERS - 1,)),
            dma((PEERS - 1,)),
            dma((3,)),
            dma((2 * groups,)),
        ],
        compiler_params=pltpu.CompilerParams(
            collective_id=0, has_side_effects=True, vmem_limit_bytes=40 * 1024 * 1024
        ),
        name="chebyshev",
    )(
        features,
        jnp.transpose(lap_tiles, (1, 0, 2)),
        columns.T,
        weights,
        bias_term.reshape(1, chan),
        cotangent,
    )
    return output, input_grad, weight_grad, bias_grad.reshape(chan)


def solution(mesh):
    split = ("patch", "strip")
    in_specs = (P(split, None), P(split, None, None), P(split, None), P(), P(), P(split, None))
    out_specs = (P(split, None), P(split, None), P(), P())
    return jax.shard_map(shards, mesh=mesh, in_specs=in_specs, out_specs=out_specs, check_vma=False)
```

time: 180 us -> 38.6 us (0.21)
  local copies, waits for them, and re-layouts: 55.3 us -> 8.46 us
  matrix products: 43.4 us -> 0 us
  blocking collectives: 38 us -> 0 us
  Pallas kernels: 0 us -> 29.2 us
  starting transfers between devices: 22.4 us -> 0 us
  other arithmetic: 17.9 us -> 0 us
    psum x1 -> x0, blocking collectives: 38 us -> none  [shards(): lax.psum((weight_local, bias_local), ('patch', 'strip'))]
    dot_general x11 -> x0, matrix products: 35.6 us -> none  [the longest x2 15.4 us: lap_rows(): return jnp.einsum('bjpq,bjqf->bpf', tile_mats, picked, precision=highest)]
    pallas_call x0 -> x1, Pallas kernels: none -> 29.2 us  [shards(): pl.pallas_call(functools.partial(body, (nb, pb, blocks, hb, blocks * devi...]
    ppermute x8 -> x0, starting transfers between devices: 22.4 us -> none  [the longest x4 11.7 us: passed_along(): lax.ppermute(value, axis, [(i, (i + by) % peers) for i in range(peers)])]
    reshape x6 -> x0, local copies, waits for them, and re-layouts: 12.9 us -> none  [the longest x4 6.98 us: shards(): map_rows = cheb_terms[order_index].reshape(row_count, BATCH, C)]
    slice x9 -> x0, local copies, waits for them, and re-layouts: 11.9 us -> none  [the longest x2 4.87 us: transposed(): own_part = spread[HB:BLK_DEV + HB]]
    unnamed x2 -> x0, matrix products: 7.83 us -> none
    scatter-add x4 -> x0, other arithmetic: 7.42 us -> none  [the longest x2 3.9 us: transposed(): return own_part.at[BLK_DEV - HB:].add(from_next)]
  transfers between devices with their start and end apart: 8 -> 0, of which waited for: 0 -> 0; matrix products, arithmetic and copies ran while one was open for 32% -> 0% of each run, Pallas kernels for 0% -> 0%
where the time goes in v1:
time: 38.6 us; the launch traced here: 38.3 us
  Pallas kernels  29.2 us (76%)
  local copies, waits for them, and re-layouts  8.46 us (22%)
  between operations  0.66 us (2%)
    pallas_call x1, Pallas kernels, shards(): pl.pallas_call(functools.partial(body, (nb, pb, blocks, hb, blocks * devi...  29.2 us
    unnamed x16, local copies, waits for them, and re-layouts  8.46 us

profile of v1, /device:TPU:0, one launch (start us, length us, event | category | flops | bytes accessed | tf_op | source)
XLA Modules:
  0.0 38.3 jit_solution(300337005312410423)
XLA Ops:
  0.6 0.0 copy-start
  0.6 1.4 %copy-done = f32[16,6,4096]{2,0,1:T(8,128)S(1)} copy-done((f32[16,6,4096]{2,0,1:T(8,128)S(1)}, f32[16,6,4096]{2,0,1:T(8,128)}, u32[]{:S(2)}) %copy-start) | copy-done | bytes 1572888
  2.0 0.0 copy-start.1
  2.0 1.0 %copy-done.1 = f32[1024,128]{1,0:T(8,128)S(1)} copy-done((f32[1024,128]{1,0:T(8,128)S(1)}, f32[1024,128]{1,0:T(8,128)}, u32[]{:S(2)}) %copy-start.1) | copy-done | bytes 524312
  3.1 0.0 copy-start.2
  3.1 1.0 %copy-done.2 = f32[1024,128]{1,0:T(8,128)S(1)} copy-done((f32[1024,128]{1,0:T(8,128)S(1)}, f32[1024,128]{1,0:T(8,128)}, u32[]{:S(2)}) %copy-start.2) | copy-done | bytes 524312
  4.1 0.0 copy-start.3
  4.1 0.9 %copy-done.3 = f32[3,64,64]{2,1,0:T(8,128)S(1)} copy-done((f32[3,64,64]{2,1,0:T(8,128)S(1)}, f32[3,64,64]{2,1,0:T(8,128)}, u32[]{:S(2)}) %copy-start.3) | copy-done | bytes 49176
  5.0 0.0 copy-start.4
  5.0 0.7 %copy-done.4 = s32[16,6]{0,1:T(8,128)S(1)} copy-done((s32[16,6]{0,1:T(8,128)S(1)}, s32[16,6]{0,1:T(8,128)}, u32[]{:S(2)}) %copy-start.4) | copy-done | bytes 408
  5.7 0.0 copy-start.5
  5.7 0.7 %copy-done.5 = f32[64]{0:T(128)S(1)} copy-done((f32[64]{0:T(128)S(1)}, f32[64]{0:T(128)}, u32[]{:S(2)}) %copy-start.5) | copy-done | bytes 280
  6.4 29.2 %chebyshev.1 = (f32[1024,128]{1,0:T(8,128)S(1)}, f32[1024,128]{1,0:T(8,128)S(1)}, f32[3,64,64]{2,1,0:T(8,128)S(1)}, f32[1,64]{1,0:T(1,128)S(1)}) custom-call(f32[1024,128]{1,0:T(8,128)S(1)} %copy-done.1, f32[6,16,4096]{2,1,0:T(8,128)S(1)} %bitcast.4, s32[6,16]{1,0:T(8,128)S(1)} %bitcast.5, f32[3,64,64]{2,1,0:T(8,128)S(1)} %copy-done.3, f32[1,64]{1,0:T(1,128)S(1)} %bitcast.6, ...), custom_call_target="tpu_custom_call" | custom-call | tf_op jit(solution)/shard_map/chebyshev/pallas_call | solution.py:354
  35.6 0.8 %copy.14 = f32[1024,128]{1,0:T(8,128)} copy(f32[1024,128]{1,0:T(8,128)S(1)} %get-tuple-element.16) | data formatting | bytes 1048576
  36.4 0.8 %copy.15 = f32[1024,128]{1,0:T(8,128)} copy(f32[1024,128]{1,0:T(8,128)S(1)} %get-tuple-element.17) | data formatting | bytes 1048576
  37.2 0.6 %copy.16 = f32[3,64,64]{2,1,0:T(8,128)} copy(f32[3,64,64]{2,1,0:T(8,128)S(1)} %get-tuple-element.18) | data formatting | bytes 98304
  37.8 0.5 %copy.17 = f32[64]{0:T(128)} copy(f32[64]{0:T(128)S(1)} %bitcast.7) | data formatting | bytes 512
Async XLA Ops:
  0.6 1.4 %copy-start = (f32[16,6,4096]{2,0,1:T(8,128)S(1)}, f32[16,6,4096]{2,0,1:T(8,128)}, u32[]{:S(2)}) copy-start(f32[16,6,4096]{2,0,1:T(8,128)} %param.7) | copy-start | bytes 4718596
  2.0 1.0 %copy-start.1 = (f32[1024,128]{1,0:T(8,128)S(1)}, f32[1024,128]{1,0:T(8,128)}, u32[]{:S(2)}) copy-start(f32[1024,128]{1,0:T(8,128)} %f_hbm.1) | copy-start | bytes 1572868
  3.1 1.0 %copy-start.2 = (f32[1024,128]{1,0:T(8,128)S(1)}, f32[1024,128]{1,0:T(8,128)}, u32[]{:S(2)}) copy-start(f32[1024,128]{1,0:T(8,128)} %cot_hbm.1) | copy-start | bytes 1572868
  4.1 0.9 %copy-start.3 = (f32[3,64,64]{2,1,0:T(8,128)S(1)}, f32[3,64,64]{2,1,0:T(8,128)}, u32[]{:S(2)}) copy-start(f32[3,64,64]{2,1,0:T(8,128)} %w_ref.1) | copy-start | bytes 147460
  5.0 0.7 %copy-start.4 = (s32[16,6]{0,1:T(8,128)S(1)}, s32[16,6]{0,1:T(8,128)}, u32[]{:S(2)}) copy-start(s32[16,6]{0,1:T(8,128)} %param.8) | copy-start | bytes 1156
  5.7 0.7 %copy-start.5 = (f32[64]{0:T(128)S(1)}, f32[64]{0:T(128)}, u32[]{:S(2)}) copy-start(f32[64]{0:T(128)} %param.10) | copy-start | bytes 772

commit v2 on v1

--- a/solution.py
+++ b/solution.py
@@ -39,12 +39,12 @@
 
 def body(
     dims,
-    f_hbm, lap_hbm, col, w_ref, b_ref, cot_hbm,
-    out_hbm, ig_hbm, wg_ref, bg_ref,
-    f_v, cot_v, lap_v, y, dhi, dlo, fc, tc, cc, uc, wf, wb, out_v, ig_v,
+    f_hbm, lap_hbm, col_hbm, w_hbm, b_hbm, cot_hbm,
+    out_v, ig_v, wg_ref, bg_ref,
+    f_v, cot_v, lap_v, col, w_ref, b_ref, y, dhi, dlo, fc, tc, cc, uc, wf, wb,
     f_in, t_in, u_in, v_in, t_out, u_out, v_out,
     grads, part_in, seg, cross, final,
-    send, recv, a_send, a_recv, b_send, b_recv, c_send, c_recv, local, put,
+    send, recv, a_send, a_recv, b_send, b_recv, c_send, c_recv, local,
 ):
     nb, pb, blocks, hb, total, scale = dims
     half, width = hb * pb, f_v.shape[1]
@@ -71,13 +71,14 @@
     greeted += [at(t * PEERS + rank) for t in others]
     for device in greeted:
         pl.semaphore_signal(barrier, inc=1, device_id=device, device_id_type=MESH)
-    load_lap = pltpu.make_async_copy(lap_hbm, lap_v, local.at[0])
-    load_cot = pltpu.make_async_copy(cot_hbm, cot_v, local.at[1])
-    load_f = pltpu.make_async_copy(f_hbm, f_v, local.at[2])
-    load_lap.start()
-    load_cot.start()
-    load_f.start()
-    pl.semaphore_wait(barrier, len(greeted))
+    loads = []
+    for src, dst in (
+        (lap_hbm, lap_v), (col_hbm, col), (cot_hbm, cot_v), (f_hbm, f_v),
+        (w_hbm, w_ref), (b_hbm, b_ref),
+    ):
+        loads.append(pltpu.make_async_copy(src, dst, local.at[len(loads)]))
+        loads[-1].start()
+    load_lap, load_col, load_cot, load_f, load_w, load_b = loads
 
     def swap(slot, to_next, to_prev, landing):
         pair = []
@@ -94,8 +95,6 @@
             pair.append(copy)
         return pair
 
-    f_swap = swap(0, f_hbm.at[pl.ds(rows - half, half)], f_hbm.at[pl.ds(0, half)], f_in)
-
     load_lap.wait()
     low = lax.broadcasted_iota(jnp.int32, (8, 128), 1) < pb
 
@@ -104,14 +103,17 @@
             for r in range(pb // 2):
                 x = lap_v[j, pl.ds(8 * eight, 8), pl.ds(128 * r, 128)]
                 turned = pltpu.roll(x, 64, 1)
-                start = 8 * eight * nb * pb + j * pb + 2 * r
-                y[pl.ds(start, 8, stride=nb * pb), :] = jnp.where(low, x, turned)
-                y[pl.ds(start + 1, 8, stride=nb * pb), :] = jnp.where(low, turned, x)
+                start = 8 * eight * apart + j * pb + 2 * r
+                y[pl.ds(start, 8, stride=apart), :] = jnp.where(low, x, turned)
+                y[pl.ds(start + 1, 8, stride=apart), :] = jnp.where(low, turned, x)
         return carry
 
+    apart = nb * pb + 8
     lax.fori_loop(0, nb, spread, 0)
-
-    side = lax.broadcasted_iota(jnp.int32, (pb, 128), 1) // pb
+    pl.semaphore_wait(barrier, len(greeted))
+    f_swap = swap(0, f_hbm.at[pl.ds(rows - half, half)], f_hbm.at[pl.ds(0, half)], f_in)
+
+    side = lax.broadcasted_iota(jnp.int32, (8, 128), 1) // pb
 
     def band(g, carry):
         for i in range(hb):
@@ -129,15 +131,17 @@
                     dhi[own, columns] = jnp.zeros((pb, 128), bf16)
                     dlo[own, columns] = jnp.zeros((pb, 128), bf16)
                     continue
-                picked = jnp.zeros((pb, 128), f32)
+                picked = jnp.zeros((pb // 8, 8, 128), f32)
                 for j in range(nb):
-                    tile = y[pl.ds(pl.multiple_of((b * nb + j) * pb, pb), pb), :]
-                    picked = jnp.where(side + 2 * m == spots[j], tile, picked)
-                hi, lo = halves(picked)
+                    tile = y[pl.ds(pl.multiple_of(b * apart + j * pb, 8), pb), :]
+                    here = jnp.broadcast_to((side == spots[j] - 2 * m)[None], picked.shape)
+                    picked = jnp.where(here, tile.reshape(picked.shape), picked)
+                hi, lo = halves(picked.reshape(pb, 128))
                 dhi[own, columns] = hi
                 dlo[own, columns] = lo
         return carry
 
+    load_col.wait()
     lax.fori_loop(0, 2, lambda t, carry: band(t * (groups - 1), carry), 0)
 
     load_cot.wait()
@@ -165,6 +169,20 @@
     u_swap = swap(1, u_out.at[0], u_out.at[1], u_in)
 
     lax.fori_loop(1, groups - 1, band, 0)
+    load_w.wait()
+    load_b.wait()
+    w0, w1, w2 = w_ref[0], w_ref[1], w_ref[2]
+    for k, mixing in enumerate((w0 - w2, w1, 2.0 * w2)):
+        hi, lo = halves(both_maps(mixing))
+        zero = jnp.zeros_like(lo)
+        wf[k] = jnp.concatenate(
+            [jnp.concatenate([hi, lo], axis=1), jnp.concatenate([hi, zero], axis=1)], axis=0
+        )
+        wb[k] = jnp.concatenate(
+            [jnp.concatenate([hi, hi], axis=1), jnp.concatenate([lo, zero], axis=1)], axis=0
+        )
+    bias = jnp.concatenate([b_ref[...], b_ref[...]], axis=1)
+
     load_f.wait()
     fc[pl.ds(half, rows), :] = side_by_side(f_v[...])
 
@@ -225,28 +243,12 @@
         copy.start()
         a_copies.append(copy)
 
-    w0, w1, w2 = w_ref[0], w_ref[1], w_ref[2]
-    for k, mixing in enumerate((w0 - w2, w1, 2.0 * w2)):
-        hi, lo = halves(both_maps(mixing))
-        zero = jnp.zeros_like(lo)
-        wf[k] = jnp.concatenate(
-            [jnp.concatenate([hi, lo], axis=1), jnp.concatenate([hi, zero], axis=1)], axis=0
-        )
-        wb[k] = jnp.concatenate(
-            [jnp.concatenate([hi, hi], axis=1), jnp.concatenate([lo, zero], axis=1)], axis=0
-        )
-    bias = jnp.concatenate([b_ref[...], b_ref[...]], axis=1)
-    puts = []
-
     def finish_out(g):
         own = pl.ds((g + 1) * half, half)
         both = dot(fc[own, :], wf[0]) + dot(tc[own, :], wf[1])
         both = both + dot(side_by_side(hop(g, tc)), wf[2])
         here = pl.ds(g * half, half)
         out_v[here, :] = both[:, :width] + both[:, width:] + bias
-        copy = pltpu.make_async_copy(out_v.at[here], out_hbm.at[here], put.at[g])
-        copy.start()
-        puts.append(copy)
 
     def finish_grad(g, arrived):
         here = pl.ds(g * half, half)
@@ -255,11 +257,9 @@
             second = second + arrived
         both = dot(wb[0], cc[:, here]) + dot(wb[1], uc[:, here]) + dot(wb[2], stacked(second))
         ig_v[here, :] = (both[:width] + both[width:]).T
-        copy = pltpu.make_async_copy(ig_v.at[here], ig_hbm.at[here], put.at[groups + g])
-        copy.start()
-        puts.append(copy)
-
-    for g in range(1, groups - 1):
+
+    middle = list(range(1, groups - 1))
+    for g in middle[:1]:
         finish_out(g)
         finish_grad(g, None)
 
@@ -283,12 +283,14 @@
         copy.start()
         b_copies.append(copy)
 
+    for g in middle[1:]:
+        finish_out(g)
+        finish_grad(g, None)
     for copy in t_swap:
         copy.wait_recv()
     tc[pl.ds(0, half), :] = side_by_side(t_in[0])
     tc[pl.ds(half + rows, half), :] = side_by_side(t_in[1])
     finish_out(0)
-    finish_out(groups - 1)
 
     for copy in b_copies:
         copy.wait_recv()
@@ -313,6 +315,7 @@
         copy.start()
         c_copies.append(copy)
 
+    finish_out(groups - 1)
     for copy in v_swap:
         copy.wait_recv()
     finish_grad(0, v_in[0])
@@ -332,7 +335,16 @@
 
     for copy in f_swap + u_swap + t_swap + v_swap + a_copies + c_copies:
         copy.wait_send()
-    for copy in puts:
+
+
+def store(*refs):
+    count = len(refs) // 2
+    done = refs[-1]
+    copies = []
+    for i in range(count):
+        copies.append(pltpu.make_async_copy(refs[i], refs[count + i], done.at[i]))
+        copies[-1].start()
+    for copy in copies:
         copy.wait()
 
 
@@ -346,33 +358,29 @@
     devices = lax.axis_size("patch") * lax.axis_size("strip")
     teams = devices // PEERS
     rim = 2 * chan // PEERS
-    groups = blocks // hb
     scale = 1.0 / math.sqrt(2 * rows * devices)
     vmem = pl.BlockSpec(memory_space=pltpu.VMEM)
-    any_space = pl.BlockSpec(memory_space=pl.ANY)
+    hbm = pl.BlockSpec(memory_space=pltpu.HBM)
     dma = pltpu.SemaphoreType.DMA
-    output, input_grad, weight_grad, bias_grad = pl.pallas_call(
+    out_shape = (
+        jax.ShapeDtypeStruct((rows, width), f32),
+        jax.ShapeDtypeStruct((rows, width), f32),
+        jax.ShapeDtypeStruct((3, chan, chan), f32),
+        jax.ShapeDtypeStruct((1, chan), f32),
+    )
+    results = pl.pallas_call(
         functools.partial(body, (nb, pb, blocks, hb, blocks * devices, scale)),
-        out_shape=(
-            jax.ShapeDtypeStruct((rows, width), f32),
-            jax.ShapeDtypeStruct((rows, width), f32),
-            jax.ShapeDtypeStruct((3, chan, chan), f32),
-            jax.ShapeDtypeStruct((1, chan), f32),
-        ),
-        in_specs=[
-            any_space,
-            any_space,
-            pl.BlockSpec(memory_space=pltpu.SMEM),
-            vmem,
-            vmem,
-            any_space,
-        ],
-        out_specs=(any_space, any_space, vmem, vmem),
+        out_shape=tuple(pltpu.VMEM(leaf.shape, leaf.dtype) for leaf in out_shape),
+        in_specs=[hbm] * 6,
+        out_specs=(vmem,) * 4,
         scratch_shapes=[
             pltpu.VMEM((rows, width), f32),
             pltpu.VMEM((rows, width), f32),
             pltpu.VMEM((nb, blocks, tile), f32),
-            pltpu.VMEM((blocks * nb * pb, 128), f32),
+            pltpu.SMEM((nb, blocks), jnp.int32),
+            pltpu.VMEM((3, chan, chan), f32),
+            pltpu.VMEM((1, chan), f32),
+            pltpu.VMEM((blocks * (nb * pb + 8), 128), f32),
             pltpu.VMEM((rows, 3 * half), bf16),
             pltpu.VMEM((rows, 3 * half), bf16),
             pltpu.VMEM((rows + 2 * half, 2 * width), bf16),
@@ -381,8 +389,6 @@
             pltpu.VMEM((2 * width, rows), bf16),
             pltpu.VMEM((3, 2 * width, 2 * width), bf16),
             pltpu.VMEM((3, 2 * width, 2 * width), bf16),
-            pltpu.VMEM((rows, width), f32),
-            pltpu.VMEM((rows, width), f32),
             pltpu.VMEM((2, half, width), f32),
             pltpu.VMEM((2, half, width), f32),
             pltpu.VMEM((2, width, half), f32),
@@ -403,11 +409,10 @@
             dma((teams - 1,)),
             dma((PEERS - 1,)),
             dma((PEERS - 1,)),
-            dma((3,)),
-            dma((2 * groups,)),
+            dma((6,)),
         ],
         compiler_params=pltpu.CompilerParams(
-            collective_id=0, has_side_effects=True, vmem_limit_bytes=40 * 1024 * 1024
+            collective_id=0, has_side_effects=True, vmem_limit_bytes=60 * 1024 * 1024
         ),
         name="chebyshev",
     )(
@@ -418,6 +423,14 @@
         bias_term.reshape(1, chan),
         cotangent,
     )
+    output, input_grad, weight_grad, bias_grad = pl.pallas_call(
+        store,
+        out_shape=out_shape,
+        in_specs=[vmem] * 4,
+        out_specs=(hbm,) * 4,
+        scratch_shapes=[dma((4,))],
+        name="store",
+    )(*results)
     return output, input_grad, weight_grad, bias_grad.reshape(chan)
 
 

time: 38.6 us -> 34.3 us (0.89)
  local copies, waits for them, and re-layouts: 8.46 us -> 2.71 us
  Pallas kernels: 29.2 us -> 30.7 us
    unnamed x16 -> x8, local copies, waits for them, and re-layouts: 8.46 us -> 2.71 us
    pallas_call x0 -> x1, Pallas kernels: none -> 2.23 us  [shards(): pl.pallas_call(store, out_shape=out_shape, in_specs=[vmem] * 4, out_specs...]
    pallas_call x1, Pallas kernels: 29.2 us -> 28.5 us  [shards(): pl.pallas_call(functools.partial(body, (nb, pb, blocks, hb, blocks * devi...]
where the time goes in v2:
time: 34.3 us; the launch traced here: 34.1 us
  Pallas kernels  30.7 us (90%)
  local copies, waits for them, and re-layouts  2.71 us (8%)
  between operations  0.65 us (2%)
    pallas_call x1, Pallas kernels, shards(): pl.pallas_call(functools.partial(body, (nb, pb, blocks, hb, blocks * devi...  28.5 us
    unnamed x8, local copies, waits for them, and re-layouts  2.71 us
    pallas_call x1, Pallas kernels, shards(): pl.pallas_call(store, out_shape=out_shape, in_specs=[vmem] * 4, out_specs...  2.23 us

profile of v2, /device:TPU:0, one launch (start us, length us, event | category | flops | bytes accessed | tf_op | source)
XLA Modules:
  0.0 34.1 jit_solution(2128845097396698948)
XLA Ops:
  0.6 28.5 %chebyshev.1 = (f32[1024,128]{1,0:T(8,128)S(1)}, f32[1024,128]{1,0:T(8,128)S(1)}, f32[3,64,64]{2,1,0:T(8,128)S(1)}, f32[1,64]{1,0:T(1,128)S(1)}) custom-call(f32[1024,128]{1,0:T(8,128)} %f_hbm.1, f32[6,16,4096]{2,1,0:T(8,128)} %bitcast.4, s32[6,16]{1,0:T(8,128)} %bitcast.5, f32[3,64,64]{2,1,0:T(8,128)} %w_hbm.1, f32[1,64]{1,0:T(1,128)} %bitcast.6, ...), custom_call_target="tpu_custom_call" | custom-call | tf_op jit(solution)/shard_map/chebyshev/pallas_call | solution.py:371
  29.1 0.0 copy-start
  29.2 0.8 %copy-done = f32[1024,128]{1,0:T(8,128)} copy-done((f32[1024,128]{1,0:T(8,128)}, f32[1024,128]{1,0:T(8,128)S(1)}, u32[]{:S(2)}) %copy-start) | copy-done | bytes 524312
  29.9 0.0 copy-start.1
  29.9 0.8 %copy-done.1 = f32[1024,128]{1,0:T(8,128)} copy-done((f32[1024,128]{1,0:T(8,128)}, f32[1024,128]{1,0:T(8,128)S(1)}, u32[]{:S(2)}) %copy-start.1) | copy-done | bytes 524312
  30.7 0.0 copy-start.2
  30.7 0.6 %copy-done.2 = f32[3,64,64]{2,1,0:T(8,128)} copy-done((f32[3,64,64]{2,1,0:T(8,128)}, f32[3,64,64]{2,1,0:T(8,128)S(1)}, u32[]{:S(2)}) %copy-start.2) | copy-done | bytes 49176
  31.4 0.0 copy-start.3
  31.4 0.5 %copy-done.3 = f32[1,64]{1,0:T(1,128)} copy-done((f32[1,64]{1,0:T(1,128)}, f32[1,64]{1,0:T(1,128)S(1)}, u32[]{:S(2)}) %copy-start.3) | copy-done | bytes 280
  31.9 2.2 %store.1 = (f32[1024,128]{1,0:T(8,128)}, f32[1024,128]{1,0:T(8,128)}, f32[3,64,64]{2,1,0:T(8,128)}, f32[1,64]{1,0:T(1,128)}) custom-call(f32[1024,128]{1,0:T(8,128)} %copy-done, f32[1024,128]{1,0:T(8,128)} %copy-done.1, f32[3,64,64]{2,1,0:T(8,128)} %copy-done.2, f32[1,64]{1,0:T(1,128)} %copy-done.3), custom_call_target="tpu_custom_call" | custom-call | tf_op jit(solution)/shard_map/store/pallas_call | solution.py:426
Async XLA Ops:
  29.1 0.8 %copy-start = (f32[1024,128]{1,0:T(8,128)}, f32[1024,128]{1,0:T(8,128)S(1)}, u32[]{:S(2)}) copy-start(f32[1024,128]{1,0:T(8,128)S(1)} %get-tuple-element.12.refs_0_) | copy-start | bytes 1572868
  29.9 0.8 %copy-start.1 = (f32[1024,128]{1,0:T(8,128)}, f32[1024,128]{1,0:T(8,128)S(1)}, u32[]{:S(2)}) copy-start(f32[1024,128]{1,0:T(8,128)S(1)} %get-tuple-element.13.refs_1_) | copy-start | bytes 1572868
  30.7 0.6 %copy-start.2 = (f32[3,64,64]{2,1,0:T(8,128)}, f32[3,64,64]{2,1,0:T(8,128)S(1)}, u32[]{:S(2)}) copy-start(f32[3,64,64]{2,1,0:T(8,128)S(1)} %get-tuple-element.14.refs_2_) | copy-start | bytes 147460
  31.4 0.5 %copy-start.3 = (f32[1,64]{1,0:T(1,128)}, f32[1,64]{1,0:T(1,128)S(1)}, u32[]{:S(2)}) copy-start(f32[1,64]{1,0:T(1,128)S(1)} %get-tuple-element.15.refs_3_) | copy-start | bytes 772

commit v3 on v2

--- a/solution.py
+++ b/solution.py
@@ -40,11 +40,12 @@
 def body(
     dims,
     f_hbm, lap_hbm, col_hbm, w_hbm, b_hbm, cot_hbm,
+    out_hbm, ig_hbm, wg_hbm, bg_hbm,
+    f_v, cot_v, lap_v, col, w_ref, b_ref, y, dhi, dlo, fc, tc, cc, uc, wf, wb,
     out_v, ig_v, wg_ref, bg_ref,
-    f_v, cot_v, lap_v, col, w_ref, b_ref, y, dhi, dlo, fc, tc, cc, uc, wf, wb,
     f_in, t_in, u_in, v_in, t_out, u_out, v_out,
     grads, part_in, seg, cross, final,
-    send, recv, a_send, a_recv, b_send, b_recv, c_send, c_recv, local,
+    send, recv, a_send, a_recv, b_send, b_recv, c_send, c_recv, local, tiles, put,
 ):
     nb, pb, blocks, hb, total, scale = dims
     half, width = hb * pb, f_v.shape[1]
@@ -73,12 +74,15 @@
         pl.semaphore_signal(barrier, inc=1, device_id=device, device_id_type=MESH)
     loads = []
     for src, dst in (
-        (lap_hbm, lap_v), (col_hbm, col), (cot_hbm, cot_v), (f_hbm, f_v),
-        (w_hbm, w_ref), (b_hbm, b_ref),
+        (cot_hbm, cot_v), (col_hbm, col), (w_hbm, w_ref), (b_hbm, b_ref), (f_hbm, f_v)
     ):
         loads.append(pltpu.make_async_copy(src, dst, local.at[len(loads)]))
-        loads[-1].start()
-    load_lap, load_col, load_cot, load_f, load_w, load_b = loads
+    load_cot, load_col, load_w, load_b, load_f = loads
+    load_cot.start()
+    for j in range(nb):
+        pltpu.make_async_copy(lap_hbm.at[j], lap_v.at[j], tiles.at[j]).start()
+    for copy in loads[1:]:
+        copy.start()
 
     def swap(slot, to_next, to_prev, landing):
         pair = []
@@ -95,10 +99,30 @@
             pair.append(copy)
         return pair
 
-    load_lap.wait()
+    load_cot.wait()
+    for g in range(groups):
+        cc[:, pl.ds(g * half, half)] = stacked(cot_v[pl.ds(g * half, half), :].T)
+
+    load_w.wait()
+    load_b.wait()
+    w0, w1, w2 = w_ref[0], w_ref[1], w_ref[2]
+    for k, mixing in enumerate((w0 - w2, w1, 2.0 * w2)):
+        hi, lo = halves(both_maps(mixing))
+        zero = jnp.zeros_like(lo)
+        wf[k] = jnp.concatenate(
+            [jnp.concatenate([hi, lo], axis=1), jnp.concatenate([hi, zero], axis=1)], axis=0
+        )
+        wb[k] = jnp.concatenate(
+            [jnp.concatenate([hi, hi], axis=1), jnp.concatenate([lo, zero], axis=1)], axis=0
+        )
+    bias = jnp.concatenate([b_ref[...], b_ref[...]], axis=1)
+    load_f.wait()
+    fc[pl.ds(half, rows), :] = side_by_side(f_v[...])
+
     low = lax.broadcasted_iota(jnp.int32, (8, 128), 1) < pb
 
     def spread(j, carry):
+        pltpu.make_async_copy(lap_hbm.at[j], lap_v.at[j], tiles.at[j]).wait()
         for eight in range(blocks // 8):
             for r in range(pb // 2):
                 x = lap_v[j, pl.ds(8 * eight, 8), pl.ds(128 * r, 128)]
@@ -144,10 +168,6 @@
     load_col.wait()
     lax.fori_loop(0, 2, lambda t, carry: band(t * (groups - 1), carry), 0)
 
-    load_cot.wait()
-    for g in range(groups):
-        cc[:, pl.ds(g * half, half)] = stacked(cot_v[pl.ds(g * half, half), :].T)
-
     def hop(g, field):
         own = pl.ds(g * half, half)
         near = field[pl.ds(g * half, 3 * half), :]
@@ -169,22 +189,6 @@
     u_swap = swap(1, u_out.at[0], u_out.at[1], u_in)
 
     lax.fori_loop(1, groups - 1, band, 0)
-    load_w.wait()
-    load_b.wait()
-    w0, w1, w2 = w_ref[0], w_ref[1], w_ref[2]
-    for k, mixing in enumerate((w0 - w2, w1, 2.0 * w2)):
-        hi, lo = halves(both_maps(mixing))
-        zero = jnp.zeros_like(lo)
-        wf[k] = jnp.concatenate(
-            [jnp.concatenate([hi, lo], axis=1), jnp.concatenate([hi, zero], axis=1)], axis=0
-        )
-        wb[k] = jnp.concatenate(
-            [jnp.concatenate([hi, hi], axis=1), jnp.concatenate([lo, zero], axis=1)], axis=0
-        )
-    bias = jnp.concatenate([b_ref[...], b_ref[...]], axis=1)
-
-    load_f.wait()
-    fc[pl.ds(half, rows), :] = side_by_side(f_v[...])
 
     for copy in f_swap:
         copy.wait_recv()
@@ -196,6 +200,10 @@
         tc[pl.ds((g + 1) * half, half), :] = side_by_side(first_term)
     t_swap = swap(2, t_out.at[0], t_out.at[1], t_in)
 
+    for g in range(1, groups - 1):
+        tc[pl.ds((g + 1) * half, half), :] = side_by_side(hop(g, fc))
+        uc[:, pl.ds(g * half, half)] = stacked(back_hop(g + 1, cc))
+
     for copy in u_swap:
         copy.wait_recv()
     for slot, k in ((0, 1), (1, groups)):
@@ -203,10 +211,6 @@
     v_out[0] = back_hop(groups + 1, uc)
     v_out[1] = back_hop(0, uc)
     v_swap = swap(3, v_out.at[0], v_out.at[1], v_in)
-
-    for g in range(1, groups - 1):
-        tc[pl.ds((g + 1) * half, half), :] = side_by_side(hop(g, fc))
-        uc[:, pl.ds(g * half, half)] = stacked(back_hop(g + 1, cc))
 
     def share(left, right):
         whole = dot(left[...], right[pl.ds(half, rows), :])
@@ -243,12 +247,20 @@
         copy.start()
         a_copies.append(copy)
 
+    puts = []
+
+    def write(src, dst):
+        copy = pltpu.make_async_copy(src, dst, put.at[len(puts)])
+        copy.start()
+        puts.append(copy)
+
     def finish_out(g):
         own = pl.ds((g + 1) * half, half)
         both = dot(fc[own, :], wf[0]) + dot(tc[own, :], wf[1])
         both = both + dot(side_by_side(hop(g, tc)), wf[2])
         here = pl.ds(g * half, half)
         out_v[here, :] = both[:, :width] + both[:, width:] + bias
+        write(out_v.at[here], out_hbm.at[here])
 
     def finish_grad(g, arrived):
         here = pl.ds(g * half, half)
@@ -257,11 +269,11 @@
             second = second + arrived
         both = dot(wb[0], cc[:, here]) + dot(wb[1], uc[:, here]) + dot(wb[2], stacked(second))
         ig_v[here, :] = (both[:width] + both[width:]).T
+        write(ig_v.at[here], ig_hbm.at[here])
 
     middle = list(range(1, groups - 1))
-    for g in middle[:1]:
+    for g in middle:
         finish_out(g)
-        finish_grad(g, None)
 
     for copy in a_copies:
         copy.wait_recv()
@@ -283,8 +295,7 @@
         copy.start()
         b_copies.append(copy)
 
-    for g in middle[1:]:
-        finish_out(g)
+    for g in middle:
         finish_grad(g, None)
     for copy in t_swap:
         copy.wait_recv()
@@ -332,18 +343,26 @@
         else:
             wg_ref[2, pl.ds(start, rim), :] = piece[:, :chan]
     bg_ref[...] = final[PEERS // 2][:1, chan:]
+    write(wg_ref, wg_hbm)
+    write(bg_ref, bg_hbm)
 
     for copy in f_swap + u_swap + t_swap + v_swap + a_copies + c_copies:
         copy.wait_send()
+    for copy in puts:
+        copy.wait()
 
 
 def store(*refs):
     count = len(refs) // 2
     done = refs[-1]
     copies = []
-    for i in range(count):
-        copies.append(pltpu.make_async_copy(refs[i], refs[count + i], done.at[i]))
-        copies[-1].start()
+    for src, dst in zip(refs[:count], refs[count:-1]):
+        parts = 4 if src.shape[0] % 32 == 0 else 1
+        size = src.shape[0] // parts
+        for p in range(parts):
+            here = pl.ds(p * size, size)
+            copies.append(pltpu.make_async_copy(src.at[here], dst.at[here], done.at[len(copies)]))
+            copies[-1].start()
     for copy in copies:
         copy.wait()
 
@@ -359,7 +378,6 @@
     teams = devices // PEERS
     rim = 2 * chan // PEERS
     scale = 1.0 / math.sqrt(2 * rows * devices)
-    vmem = pl.BlockSpec(memory_space=pltpu.VMEM)
     hbm = pl.BlockSpec(memory_space=pltpu.HBM)
     dma = pltpu.SemaphoreType.DMA
     out_shape = (
@@ -370,9 +388,9 @@
     )
     results = pl.pallas_call(
         functools.partial(body, (nb, pb, blocks, hb, blocks * devices, scale)),
-        out_shape=tuple(pltpu.VMEM(leaf.shape, leaf.dtype) for leaf in out_shape),
+        out_shape=out_shape,
         in_specs=[hbm] * 6,
-        out_specs=(vmem,) * 4,
+        out_specs=(hbm,) * 4,
         scratch_shapes=[
             pltpu.VMEM((rows, width), f32),
             pltpu.VMEM((rows, width), f32),
@@ -389,6 +407,10 @@
             pltpu.VMEM((2 * width, rows), bf16),
             pltpu.VMEM((3, 2 * width, 2 * width), bf16),
             pltpu.VMEM((3, 2 * width, 2 * width), bf16),
+            pltpu.VMEM((rows, width), f32),
+            pltpu.VMEM((rows, width), f32),
+            pltpu.VMEM((3, chan, chan), f32),
+            pltpu.VMEM((1, chan), f32),
             pltpu.VMEM((2, half, width), f32),
             pltpu.VMEM((2, half, width), f32),
             pltpu.VMEM((2, width, half), f32),
@@ -409,10 +431,12 @@
             dma((teams - 1,)),
             dma((PEERS - 1,)),
             dma((PEERS - 1,)),
-            dma((6,)),
+            dma((5,)),
+            dma((nb,)),
+            dma((2 * (blocks // hb) + 2,)),
         ],
         compiler_params=pltpu.CompilerParams(
-            collective_id=0, has_side_effects=True, vmem_limit_bytes=60 * 1024 * 1024
+            collective_id=0, has_side_effects=True, vmem_limit_bytes=62 * 1024 * 1024
         ),
         name="chebyshev",
     )(
@@ -426,9 +450,10 @@
     output, input_grad, weight_grad, bias_grad = pl.pallas_call(
         store,
         out_shape=out_shape,
-        in_specs=[vmem] * 4,
+        in_specs=[hbm] * 4,
         out_specs=(hbm,) * 4,
-        scratch_shapes=[dma((4,))],
+        scratch_shapes=[dma((10,))],
+        compiler_params=pltpu.CompilerParams(vmem_limit_bytes=62 * 1024 * 1024),
         name="store",
     )(*results)
     return output, input_grad, weight_grad, bias_grad.reshape(chan)

time: 34.3 us -> 66.5 us (1.94)
  Pallas kernels: 30.7 us -> 65.7 us
  local copies, waits for them, and re-layouts: 2.71 us -> 0 us
    pallas_call x1, Pallas kernels: 2.23 us -> 36 us  [shards(): pl.pallas_call(store, out_shape=out_shape, in_specs=[hbm] * 4, out_specs=...]
    unnamed x8 -> x0, local copies, waits for them, and re-layouts: 2.71 us -> none
    pallas_call x1, Pallas kernels: 28.5 us -> 29.8 us  [shards(): pl.pallas_call(functools.partial(body, (nb, pb, blocks, hb, blocks * devi...]
where the time goes in v3:
time: 66.5 us; the launch traced here: 66.4 us
  Pallas kernels  65.7 us (99%)
    pallas_call x1, Pallas kernels, shards(): pl.pallas_call(store, out_shape=out_shape, in_specs=[hbm] * 4, out_specs=...  36 us
    pallas_call x1, Pallas kernels, shards(): pl.pallas_call(functools.partial(body, (nb, pb, blocks, hb, blocks * devi...  29.8 us

profile of v3, /device:TPU:0, one launch (start us, length us, event | category | flops | bytes accessed | tf_op | source)
XLA Modules:
  0.0 66.4 jit_solution(17292347364845637240)
XLA Ops:
  0.6 29.8 %chebyshev.1 = (f32[1024,128]{1,0:T(8,128)}, f32[1024,128]{1,0:T(8,128)}, f32[3,64,64]{2,1,0:T(8,128)}, f32[1,64]{1,0:T(1,128)}) custom-call(f32[1024,128]{1,0:T(8,128)} %f_hbm.1, f32[6,16,4096]{2,1,0:T(8,128)} %bitcast.4, s32[6,16]{1,0:T(8,128)} %bitcast.5, f32[3,64,64]{2,1,0:T(8,128)} %w_hbm.1, f32[1,64]{1,0:T(1,128)} %bitcast.6, f32[1024,128]{1,0:T(8,128)} %cot_hbm.1), custom_call_target="tpu_custom_call" | custom-call | tf_op jit(solution)/shard_map/chebyshev/pallas_call | solution.py:389
  30.4 36.0 %store.1 = (f32[1024,128]{1,0:T(8,128)}, f32[1024,128]{1,0:T(8,128)}, f32[3,64,64]{2,1,0:T(8,128)}, f32[1,64]{1,0:T(1,128)}) custom-call(f32[1024,128]{1,0:T(8,128)} %get-tuple-element.12.refs_0_, f32[1024,128]{1,0:T(8,128)} %get-tuple-element.13.refs_1_, f32[3,64,64]{2,1,0:T(8,128)} %get-tuple-element.14.refs_2_, f32[1,64]{1,0:T(1,128)} %get-tuple-element.15.refs_3_), custom_call_target="tpu_custom_call" | custom-call | tf_op jit(solution)/shard_map/store/pallas_call | solution.py:450

commit v4 on v3

--- a/solution.py
+++ b/solution.py
@@ -103,37 +103,24 @@
     for g in range(groups):
         cc[:, pl.ds(g * half, half)] = stacked(cot_v[pl.ds(g * half, half), :].T)
 
-    load_w.wait()
-    load_b.wait()
-    w0, w1, w2 = w_ref[0], w_ref[1], w_ref[2]
-    for k, mixing in enumerate((w0 - w2, w1, 2.0 * w2)):
-        hi, lo = halves(both_maps(mixing))
-        zero = jnp.zeros_like(lo)
-        wf[k] = jnp.concatenate(
-            [jnp.concatenate([hi, lo], axis=1), jnp.concatenate([hi, zero], axis=1)], axis=0
-        )
-        wb[k] = jnp.concatenate(
-            [jnp.concatenate([hi, hi], axis=1), jnp.concatenate([lo, zero], axis=1)], axis=0
-        )
-    bias = jnp.concatenate([b_ref[...], b_ref[...]], axis=1)
-    load_f.wait()
-    fc[pl.ds(half, rows), :] = side_by_side(f_v[...])
-
     low = lax.broadcasted_iota(jnp.int32, (8, 128), 1) < pb
-
-    def spread(j, carry):
-        pltpu.make_async_copy(lap_hbm.at[j], lap_v.at[j], tiles.at[j]).wait()
+    apart = nb * pb // 2 + 8
+
+    def spread(pair, carry):
+        for j in (2 * pair, 2 * pair + 1):
+            pltpu.make_async_copy(lap_hbm.at[j], lap_v.at[j], tiles.at[j]).wait()
         for eight in range(blocks // 8):
             for r in range(pb // 2):
-                x = lap_v[j, pl.ds(8 * eight, 8), pl.ds(128 * r, 128)]
-                turned = pltpu.roll(x, 64, 1)
-                start = 8 * eight * apart + j * pb + 2 * r
-                y[pl.ds(start, 8, stride=apart), :] = jnp.where(low, x, turned)
-                y[pl.ds(start + 1, 8, stride=apart), :] = jnp.where(low, turned, x)
+                here = (pl.ds(8 * eight, 8), pl.ds(128 * r, 128))
+                a, b = lap_v[(2 * pair, *here)], lap_v[(2 * pair + 1, *here)]
+                start = 8 * eight * apart + pair * pb + 2 * r
+                even = jnp.where(low, a, pltpu.roll(b, pb, 1))
+                odd = jnp.where(low, pltpu.roll(a, pb, 1), b)
+                y[pl.ds(start, 8, stride=apart), :] = even
+                y[pl.ds(start + 1, 8, stride=apart), :] = odd
         return carry
 
-    apart = nb * pb + 8
-    lax.fori_loop(0, nb, spread, 0)
+    lax.fori_loop(0, nb // 2, spread, 0)
     pl.semaphore_wait(barrier, len(greeted))
     f_swap = swap(0, f_hbm.at[pl.ds(rows - half, half)], f_hbm.at[pl.ds(0, half)], f_in)
 
@@ -148,21 +135,32 @@
                 d = jnp.where(d < 0, d + total, d)
                 d = jnp.where(d >= total, d - total, d)
                 spots.append(d + i)
-            own = pl.ds(pl.multiple_of(b * pb, pb), pb)
-            for m in range(3 * hb // 2):
-                columns = pl.ds(128 * m, 128)
-                if 2 * m + 1 < i or 2 * m > i + 2 * hb:
-                    dhi[own, columns] = jnp.zeros((pb, 128), bf16)
-                    dlo[own, columns] = jnp.zeros((pb, 128), bf16)
-                    continue
-                picked = jnp.zeros((pb // 8, 8, 128), f32)
-                for j in range(nb):
-                    tile = y[pl.ds(pl.multiple_of(b * apart + j * pb, 8), pb), :]
-                    here = jnp.broadcast_to((side == spots[j] - 2 * m)[None], picked.shape)
-                    picked = jnp.where(here, tile.reshape(picked.shape), picked)
-                hi, lo = halves(picked.reshape(pb, 128))
-                dhi[own, columns] = hi
-                dlo[own, columns] = lo
+            ordered, swapped = [], []
+            for pair in range(nb // 2):
+                near, far = spots[2 * pair], spots[2 * pair + 1]
+                ordered.append(jnp.where(low, near, far) - side)
+                swapped.append(jnp.where(low, far, near) - side)
+            for part in range(pb // 32):
+                own = pl.ds(pl.multiple_of(b * pb + 32 * part, 32), 32)
+                kept = []
+                for pair in range(nb // 2):
+                    start = pl.multiple_of(b * apart + pair * pb + 32 * part, 8)
+                    tile = y[pl.ds(start, 32), :]
+                    kept.append((ordered[pair], tile.reshape(4, 8, 128)))
+                    kept.append((swapped[pair], pltpu.roll(tile, pb, 1).reshape(4, 8, 128)))
+                for m in range(3 * hb // 2):
+                    columns = pl.ds(128 * m, 128)
+                    if 2 * m + 1 < i or 2 * m > i + 2 * hb:
+                        dhi[own, columns] = jnp.zeros((32, 128), bf16)
+                        dlo[own, columns] = jnp.zeros((32, 128), bf16)
+                        continue
+                    picked = jnp.zeros((4, 8, 128), f32)
+                    for spot, tile in kept:
+                        here = jnp.broadcast_to((spot == 2 * m)[None], picked.shape)
+                        picked = jnp.where(here, tile, picked)
+                    hi, lo = halves(picked.reshape(32, 128))
+                    dhi[own, columns] = hi
+                    dlo[own, columns] = lo
         return carry
 
     load_col.wait()
@@ -189,6 +187,21 @@
     u_swap = swap(1, u_out.at[0], u_out.at[1], u_in)
 
     lax.fori_loop(1, groups - 1, band, 0)
+    load_w.wait()
+    load_b.wait()
+    w0, w1, w2 = w_ref[0], w_ref[1], w_ref[2]
+    for k, mixing in enumerate((w0 - w2, w1, 2.0 * w2)):
+        hi, lo = halves(both_maps(mixing))
+        zero = jnp.zeros_like(lo)
+        wf[k] = jnp.concatenate(
+            [jnp.concatenate([hi, lo], axis=1), jnp.concatenate([hi, zero], axis=1)], axis=0
+        )
+        wb[k] = jnp.concatenate(
+            [jnp.concatenate([hi, hi], axis=1), jnp.concatenate([lo, zero], axis=1)], axis=0
+        )
+    bias = jnp.concatenate([b_ref[...], b_ref[...]], axis=1)
+    load_f.wait()
+    fc[pl.ds(half, rows), :] = side_by_side(f_v[...])
 
     for copy in f_swap:
         copy.wait_recv()
@@ -200,10 +213,6 @@
         tc[pl.ds((g + 1) * half, half), :] = side_by_side(first_term)
     t_swap = swap(2, t_out.at[0], t_out.at[1], t_in)
 
-    for g in range(1, groups - 1):
-        tc[pl.ds((g + 1) * half, half), :] = side_by_side(hop(g, fc))
-        uc[:, pl.ds(g * half, half)] = stacked(back_hop(g + 1, cc))
-
     for copy in u_swap:
         copy.wait_recv()
     for slot, k in ((0, 1), (1, groups)):
@@ -211,6 +220,10 @@
     v_out[0] = back_hop(groups + 1, uc)
     v_out[1] = back_hop(0, uc)
     v_swap = swap(3, v_out.at[0], v_out.at[1], v_in)
+
+    for g in range(1, groups - 1):
+        tc[pl.ds((g + 1) * half, half), :] = side_by_side(hop(g, fc))
+        uc[:, pl.ds(g * half, half)] = stacked(back_hop(g + 1, cc))
 
     def share(left, right):
         whole = dot(left[...], right[pl.ds(half, rows), :])
@@ -353,17 +366,23 @@
 
 
 def store(*refs):
-    count = len(refs) // 2
-    done = refs[-1]
-    copies = []
-    for src, dst in zip(refs[:count], refs[count:-1]):
+    count = 4
+    sources, targets, held = refs[:count], refs[count : 2 * count], refs[2 * count : 3 * count]
+    arrived, done = refs[3 * count :]
+    ins, outs = [], []
+    for src, dst, mid in zip(sources, targets, held):
         parts = 4 if src.shape[0] % 32 == 0 else 1
         size = src.shape[0] // parts
         for p in range(parts):
             here = pl.ds(p * size, size)
-            copies.append(pltpu.make_async_copy(src.at[here], dst.at[here], done.at[len(copies)]))
-            copies[-1].start()
-    for copy in copies:
+            k = len(ins)
+            ins.append(pltpu.make_async_copy(src.at[here], mid.at[here], arrived.at[k]))
+            outs.append(pltpu.make_async_copy(mid.at[here], dst.at[here], done.at[k]))
+            ins[-1].start()
+    for first, second in zip(ins, outs):
+        first.wait()
+        second.start()
+    for copy in outs:
         copy.wait()
 
 
@@ -398,7 +417,7 @@
             pltpu.SMEM((nb, blocks), jnp.int32),
             pltpu.VMEM((3, chan, chan), f32),
             pltpu.VMEM((1, chan), f32),
-            pltpu.VMEM((blocks * (nb * pb + 8), 128), f32),
+            pltpu.VMEM((blocks * (nb * pb // 2 + 8), 128), f32),
             pltpu.VMEM((rows, 3 * half), bf16),
             pltpu.VMEM((rows, 3 * half), bf16),
             pltpu.VMEM((rows + 2 * half, 2 * width), bf16),
@@ -452,7 +471,7 @@
         out_shape=out_shape,
         in_specs=[hbm] * 4,
         out_specs=(hbm,) * 4,
-        scratch_shapes=[dma((10,))],
+        scratch_shapes=[pltpu.VMEM(leaf.shape, f32) for leaf in out_shape] + [dma((10,))] * 2,
         compiler_params=pltpu.CompilerParams(vmem_limit_bytes=62 * 1024 * 1024),
         name="store",
     )(*results)

time: 66.5 us -> 31.8 us (0.48)
  Pallas kernels: 65.7 us -> 31 us
    pallas_call x1, Pallas kernels: 36 us -> 2.15 us  [shards(): pl.pallas_call(store, out_shape=out_shape, in_specs=[hbm] * 4, out_specs=...]
    pallas_call x1, Pallas kernels: 29.8 us -> 28.8 us  [shards(): pl.pallas_call(functools.partial(body, (nb, pb, blocks, hb, blocks * devi...]
where the time goes in v4:
time: 31.8 us; the launch traced here: 31.6 us
  Pallas kernels  31 us (97%)
  between operations  0.64 us (2%)
    pallas_call x1, Pallas kernels, shards(): pl.pallas_call(functools.partial(body, (nb, pb, blocks, hb, blocks * devi...  28.8 us
    pallas_call x1, Pallas kernels, shards(): pl.pallas_call(store, out_shape=out_shape, in_specs=[hbm] * 4, out_specs=...  2.15 us

profile of v4, /device:TPU:0, one launch (start us, length us, event | category | flops | bytes accessed | tf_op | source)
XLA Modules:
  0.0 31.6 jit_solution(10688406402024660992)
XLA Ops:
  0.6 28.8 %chebyshev.1 = (f32[1024,128]{1,0:T(8,128)}, f32[1024,128]{1,0:T(8,128)}, f32[3,64,64]{2,1,0:T(8,128)}, f32[1,64]{1,0:T(1,128)}) custom-call(f32[1024,128]{1,0:T(8,128)} %f_hbm.1, f32[6,16,4096]{2,1,0:T(8,128)} %bitcast.4, s32[6,16]{1,0:T(8,128)} %bitcast.5, f32[3,64,64]{2,1,0:T(8,128)} %w_hbm.1, f32[1,64]{1,0:T(1,128)} %bitcast.6, f32[1024,128]{1,0:T(8,128)} %cot_hbm.1), custom_call_target="tpu_custom_call" | custom-call | tf_op jit(solution)/shard_map/chebyshev/pallas_call | solution.py:408
  29.4 2.2 %store.1 = (f32[1024,128]{1,0:T(8,128)}, f32[1024,128]{1,0:T(8,128)}, f32[3,64,64]{2,1,0:T(8,128)}, f32[1,64]{1,0:T(1,128)}) custom-call(f32[1024,128]{1,0:T(8,128)} %get-tuple-element.12.refs_0_, f32[1024,128]{1,0:T(8,128)} %get-tuple-element.13.refs_1_, f32[3,64,64]{2,1,0:T(8,128)} %get-tuple-element.14.refs_2_, f32[1,64]{1,0:T(1,128)} %get-tuple-element.15.refs_3_), custom_call_target="tpu_custom_call" | custom-call | tf_op jit(solution)/shard_map/store/pallas_call | solution.py:469

commit v5 on v4

--- a/solution.py
+++ b/solution.py
@@ -103,6 +103,9 @@
     for g in range(groups):
         cc[:, pl.ds(g * half, half)] = stacked(cot_v[pl.ds(g * half, half), :].T)
 
+    pl.semaphore_wait(barrier, len(greeted))
+    f_swap = swap(0, f_hbm.at[pl.ds(rows - half, half)], f_hbm.at[pl.ds(0, half)], f_in)
+
     low = lax.broadcasted_iota(jnp.int32, (8, 128), 1) < pb
     apart = nb * pb // 2 + 8
 
@@ -121,8 +124,6 @@
         return carry
 
     lax.fori_loop(0, nb // 2, spread, 0)
-    pl.semaphore_wait(barrier, len(greeted))
-    f_swap = swap(0, f_hbm.at[pl.ds(rows - half, half)], f_hbm.at[pl.ds(0, half)], f_in)
 
     side = lax.broadcasted_iota(jnp.int32, (8, 128), 1) // pb
 
@@ -186,6 +187,18 @@
     u_out[1] = back_hop(0, cc)
     u_swap = swap(1, u_out.at[0], u_out.at[1], u_in)
 
+    load_f.wait()
+    fc[pl.ds(half, rows), :] = side_by_side(f_v[...])
+
+    for copy in f_swap:
+        copy.wait_recv()
+    fc[pl.ds(0, half), :] = side_by_side(f_in[0])
+    fc[pl.ds(half + rows, half), :] = side_by_side(f_in[1])
+    for slot, g in ((0, groups - 1), (1, 0)):
+        first_term = hop(g, fc)
+        t_out[slot] = first_term
+        tc[pl.ds((g + 1) * half, half), :] = side_by_side(first_term)
+    t_swap = swap(2, t_out.at[0], t_out.at[1], t_in)
     lax.fori_loop(1, groups - 1, band, 0)
     load_w.wait()
     load_b.wait()
@@ -200,18 +213,6 @@
             [jnp.concatenate([hi, hi], axis=1), jnp.concatenate([lo, zero], axis=1)], axis=0
         )
     bias = jnp.concatenate([b_ref[...], b_ref[...]], axis=1)
-    load_f.wait()
-    fc[pl.ds(half, rows), :] = side_by_side(f_v[...])
-
-    for copy in f_swap:
-        copy.wait_recv()
-    fc[pl.ds(0, half), :] = side_by_side(f_in[0])
-    fc[pl.ds(half + rows, half), :] = side_by_side(f_in[1])
-    for slot, g in ((0, groups - 1), (1, 0)):
-        first_term = hop(g, fc)
-        t_out[slot] = first_term
-        tc[pl.ds((g + 1) * half, half), :] = side_by_side(first_term)
-    t_swap = swap(2, t_out.at[0], t_out.at[1], t_in)
 
     for copy in u_swap:
         copy.wait_recv()

time: 31.8 us -> 31.6 us (level)
  no operation moved by 1% of the time
where the time goes in v5:
time: 31.6 us; the launch traced here: 31.4 us
  Pallas kernels  30.8 us (97%)
  between operations  0.64 us (2%)
    pallas_call x1, Pallas kernels, shards(): pl.pallas_call(functools.partial(body, (nb, pb, blocks, hb, blocks * devi...  28.6 us
    pallas_call x1, Pallas kernels, shards(): pl.pallas_call(store, out_shape=out_shape, in_specs=[hbm] * 4, out_specs=...  2.15 us

profile of v5, /device:TPU:0, one launch (start us, length us, event | category | flops | bytes accessed | tf_op | source)
XLA Modules:
  0.0 31.4 jit_solution(12238714130668121935)
XLA Ops:
  0.6 28.6 %chebyshev.1 = (f32[1024,128]{1,0:T(8,128)}, f32[1024,128]{1,0:T(8,128)}, f32[3,64,64]{2,1,0:T(8,128)}, f32[1,64]{1,0:T(1,128)}) custom-call(f32[1024,128]{1,0:T(8,128)} %f_hbm.1, f32[6,16,4096]{2,1,0:T(8,128)} %bitcast.4, s32[6,16]{1,0:T(8,128)} %bitcast.5, f32[3,64,64]{2,1,0:T(8,128)} %w_hbm.1, f32[1,64]{1,0:T(1,128)} %bitcast.6, f32[1024,128]{1,0:T(8,128)} %cot_hbm.1), custom_call_target="tpu_custom_call" | custom-call | tf_op jit(solution)/shard_map/chebyshev/pallas_call | solution.py:409
  29.3 2.2 %store.1 = (f32[1024,128]{1,0:T(8,128)}, f32[1024,128]{1,0:T(8,128)}, f32[3,64,64]{2,1,0:T(8,128)}, f32[1,64]{1,0:T(1,128)}) custom-call(f32[1024,128]{1,0:T(8,128)} %get-tuple-element.12.refs_0_, f32[1024,128]{1,0:T(8,128)} %get-tuple-element.13.refs_1_, f32[3,64,64]{2,1,0:T(8,128)} %get-tuple-element.14.refs_2_, f32[1,64]{1,0:T(1,128)} %get-tuple-element.15.refs_3_), custom_call_target="tpu_custom_call" | custom-call | tf_op jit(solution)/shard_map/store/pallas_call | solution.py:470

commit v6 on v5

--- a/solution.py
+++ b/solution.py
@@ -41,7 +41,7 @@
     dims,
     f_hbm, lap_hbm, col_hbm, w_hbm, b_hbm, cot_hbm,
     out_hbm, ig_hbm, wg_hbm, bg_hbm,
-    f_v, cot_v, lap_v, col, w_ref, b_ref, y, dhi, dlo, fc, tc, cc, uc, wf, wb,
+    f_v, cot_v, lap_v, col, w_ref, b_ref, y, dd, fc, tc, cc, uc, wf, wb,
     out_v, ig_v, wg_ref, bg_ref,
     f_in, t_in, u_in, v_in, t_out, u_out, v_out,
     grads, part_in, seg, cross, final,
@@ -142,7 +142,9 @@
                 ordered.append(jnp.where(low, near, far) - side)
                 swapped.append(jnp.where(low, far, near) - side)
             for part in range(pb // 32):
-                own = pl.ds(pl.multiple_of(b * pb + 32 * part, 32), 32)
+                top = g * 2 * half + i * pb + 32 * part
+                own = pl.ds(pl.multiple_of(top, 32), 32)
+                own_low = pl.ds(pl.multiple_of(top + half, 32), 32)
                 kept = []
                 for pair in range(nb // 2):
                     start = pl.multiple_of(b * apart + pair * pb + 32 * part, 8)
@@ -152,34 +154,33 @@
                 for m in range(3 * hb // 2):
                     columns = pl.ds(128 * m, 128)
                     if 2 * m + 1 < i or 2 * m > i + 2 * hb:
-                        dhi[own, columns] = jnp.zeros((32, 128), bf16)
-                        dlo[own, columns] = jnp.zeros((32, 128), bf16)
+                        dd[own, columns] = jnp.zeros((32, 128), bf16)
+                        dd[own_low, columns] = jnp.zeros((32, 128), bf16)
                         continue
                     picked = jnp.zeros((4, 8, 128), f32)
                     for spot, tile in kept:
                         here = jnp.broadcast_to((spot == 2 * m)[None], picked.shape)
                         picked = jnp.where(here, tile, picked)
                     hi, lo = halves(picked.reshape(32, 128))
-                    dhi[own, columns] = hi
-                    dlo[own, columns] = lo
+                    dd[own, columns] = hi
+                    dd[own_low, columns] = lo
         return carry
 
     load_col.wait()
     lax.fori_loop(0, 2, lambda t, carry: band(t * (groups - 1), carry), 0)
 
     def hop(g, field):
-        own = pl.ds(g * half, half)
-        near = field[pl.ds(g * half, 3 * half), :]
-        both = dot(dhi[own, :], near)
-        return both[:, :width] + both[:, width:] + dot(dlo[own, :], near[:, :width])
+        both = dot(dd[pl.ds(g * 2 * half, 2 * half), :], field[pl.ds(g * half, 3 * half), :])
+        return both[:half, :width] + (both[:half, width:] + both[half:, :width])
 
     def back_hop(k, field):
         total_here = None
         for g in range(max(0, k - 2), min(groups - 1, k) + 1):
             value = field[:, pl.ds(g * half, half)]
-            block = (pl.ds(g * half, half), pl.ds((k - g) * half, half))
-            both = dot(value, dhi[block])
-            term = both[:width] + both[width:] + dot(value[:width], dlo[block])
+            block = pl.ds((k - g) * half, half)
+            both = dot(value, dd[pl.ds(2 * g * half, half), block])
+            low_part = dot(value[:width], dd[pl.ds((2 * g + 1) * half, half), block])
+            term = both[:width] + both[width:] + low_part
             total_here = term if total_here is None else total_here + term
         return total_here
 
@@ -419,8 +420,7 @@
             pltpu.VMEM((3, chan, chan), f32),
             pltpu.VMEM((1, chan), f32),
             pltpu.VMEM((blocks * (nb * pb // 2 + 8), 128), f32),
-            pltpu.VMEM((rows, 3 * half), bf16),
-            pltpu.VMEM((rows, 3 * half), bf16),
+            pltpu.VMEM((2 * rows, 3 * half), bf16),
             pltpu.VMEM((rows + 2 * half, 2 * width), bf16),
             pltpu.VMEM((rows + 2 * half, 2 * width), bf16),
             pltpu.VMEM((2 * width, rows), bf16),

time: 31.6 us -> 31.7 us (level)
  no operation moved by 1% of the time
where the time goes in v6:
time: 31.7 us; the launch traced here: 31.5 us
  Pallas kernels  30.9 us (97%)
  between operations  0.64 us (2%)
    pallas_call x1, Pallas kernels, shards(): pl.pallas_call(functools.partial(body, (nb, pb, blocks, hb, blocks * devi...  28.7 us
    pallas_call x1, Pallas kernels, shards(): pl.pallas_call(store, out_shape=out_shape, in_specs=[hbm] * 4, out_specs=...  2.15 us

profile of v6, /device:TPU:0, one launch (start us, length us, event | category | flops | bytes accessed | tf_op | source)
XLA Modules:
  0.0 31.5 jit_solution(5807518539134372974)
XLA Ops:
  0.6 28.7 %chebyshev.1 = (f32[1024,128]{1,0:T(8,128)}, f32[1024,128]{1,0:T(8,128)}, f32[3,64,64]{2,1,0:T(8,128)}, f32[1,64]{1,0:T(1,128)}) custom-call(f32[1024,128]{1,0:T(8,128)} %f_hbm.1, f32[6,16,4096]{2,1,0:T(8,128)} %bitcast.4, s32[6,16]{1,0:T(8,128)} %bitcast.5, f32[3,64,64]{2,1,0:T(8,128)} %w_hbm.1, f32[1,64]{1,0:T(1,128)} %bitcast.6, f32[1024,128]{1,0:T(8,128)} %cot_hbm.1), custom_call_target="tpu_custom_call" | custom-call | tf_op jit(solution)/shard_map/chebyshev/pallas_call | solution.py:410
  29.3 2.2 %store.1 = (f32[1024,128]{1,0:T(8,128)}, f32[1024,128]{1,0:T(8,128)}, f32[3,64,64]{2,1,0:T(8,128)}, f32[1,64]{1,0:T(1,128)}) custom-call(f32[1024,128]{1,0:T(8,128)} %get-tuple-element.12.refs_0_, f32[1024,128]{1,0:T(8,128)} %get-tuple-element.13.refs_1_, f32[3,64,64]{2,1,0:T(8,128)} %get-tuple-element.14.refs_2_, f32[1,64]{1,0:T(1,128)} %get-tuple-element.15.refs_3_), custom_call_target="tpu_custom_call" | custom-call | tf_op jit(solution)/shard_map/store/pallas_call | solution.py:470
